TPU v7x, 128 devices: a whole 4x4x4 slice. The times are simulated.
128 devices in a mesh: blk: 8 (over y, x_hi), rep: 16 (over x_lo, z, core).
Axes of the slice: x: 4 (x_hi: 2, x_lo: 2; x = x_hi * 2 + x_lo), y: 4, z: 4, core: 2. Of those that a mesh axis runs over, the one named last changes fastest.
Arguments:
- features: bfloat16 [65536, 256], P(('blk', 'rep')), may hold values from -6 to 6
- adj_tiles: bfloat16 [8, 16, 512, 128, 128], P('blk', 'rep'), may hold values from 0 to 1, as said below
- tile_rows: int32 [8, 16, 512], P('blk', 'rep'), may hold values from 0 to 31
- tile_cols: int32 [8, 16, 512], P('blk', 'rep'), may hold values from 0 to 63
- tile_count: int32 [8, 16], P('blk', 'rep'), may hold values from 128 to 512
- w_neigh: bfloat16 [256, 256], replicated, may hold values from -5 to 5
- w_self: bfloat16 [256, 256], replicated, may hold values from -0.375 to 0.375
- bias: float32 [256], replicated, may hold values from -3 to 3
- out_grad: bfloat16 [65536, 256], P(('blk', 'rep')), may hold values from -6 to 6
Outputs:
- activations: bfloat16 [65536, 256], P(('blk', 'rep'))
- grad_features: bfloat16 [65536, 256], P(('blk', 'rep'))
- grad_w_neigh: float32 [256, 256], replicated
- grad_w_self: float32 [256, 256], replicated
- grad_bias: float32 [256], replicated
Inputs may be any that keep to these rules, and one draw needn't show every extreme that they name: `adj_tiles`: entries are 0 or 1.
All inputs are finite; a program needn't handle non-finite values.
Results may differ from a plain program's by a relative error of at most 0.03.
Values may be sent and summed in bfloat16 or wider, within the bound.
A program may use at most 192 MiB of HBM per device.

v0:
```python
import math

import jax
import jax.numpy as jnp
from jax import lax
from jax.sharding import PartitionSpec as P


def tile_pass(tiles, block_fn, init):
    total_slots = tiles.shape[0]
    block_size = math.gcd(total_slots, 64)
    trip_count = total_slots // block_size

    def advance(turn, carried):
        return block_fn(turn * block_size, block_size, carried)

    return lax.fori_loop(0, trip_count, advance, init)


def local(features, adj_tiles, tile_rows, tile_cols, tile_count, w_neigh, w_self, bias, out_grad):
    tiles = adj_tiles[0, 0]
    row_index = tile_rows[0, 0]
    col_index = tile_cols[0, 0]
    live_tiles = tile_count[0, 0]
    span, width = features.shape
    edge = tiles.shape[1]
    group_rows = span * lax.axis_size("blk")
    block_rows = span * lax.axis_size("rep")
    row_tiles = group_rows // edge
    col_tiles = block_rows // edge
    over_rows = (((0,), (0,)), ((), ()))
    over_cols = (((1,), (1,)), ((), ()))
    sources = lax.all_gather(features, "rep", axis=0, tiled=True).reshape(col_tiles, edge, width)

    def forward_block(start, block_size, carried):
        partial_value, degree_part = carried
        tile_block = lax.dynamic_slice_in_dim(tiles, start, block_size, 0)
        rows_here = lax.dynamic_slice_in_dim(row_index, start, block_size, 0)
        cols_here = lax.dynamic_slice_in_dim(col_index, start, block_size, 0)
        alive = (start + jnp.arange(block_size) < live_tiles).astype(jnp.float32)
        picked = sources[cols_here]
        products = jnp.einsum(
            "tij,tjd->tid", tile_block, picked, preferred_element_type=jnp.float32
        )
        row_sums = jnp.sum(tile_block.astype(jnp.float32), axis=2)
        partial_value = partial_value.at[rows_here].add(products * alive[:, None, None])
        degree_part = degree_part.at[rows_here].add(row_sums * alive[:, None])
        return (partial_value, degree_part)

    forward_init = (
        jnp.zeros((row_tiles, edge, width), jnp.float32),
        jnp.zeros((row_tiles, edge), jnp.float32),
    )
    partial_value, degree_part = tile_pass(tiles, forward_block, forward_init)
    partial_rounded = (
        partial_value.reshape(group_rows, width).astype(jnp.bfloat16).astype(jnp.float32)
    )
    aggregate = lax.psum_scatter(
        partial_rounded.astype(jnp.bfloat16), "blk", scatter_dimension=0, tiled=True
    ).astype(jnp.float32)
    degree_flat = degree_part.reshape(group_rows)
    degree = lax.psum_scatter(degree_flat, "blk", scatter_dimension=0, tiled=True)
    divisor = jnp.maximum(degree, 1.0)
    mean_rows = (aggregate / divisor[:, None]).astype(jnp.bfloat16)
    pre = jnp.dot(mean_rows, w_neigh, preferred_element_type=jnp.float32)
    pre = pre + jnp.dot(features, w_self, preferred_element_type=jnp.float32) + bias
    activations = jax.nn.silu(pre).astype(jnp.bfloat16)
    sigma = jax.nn.sigmoid(pre)
    d_pre = (out_grad.astype(jnp.float32) * sigma * (1.0 + pre * (1.0 - sigma))).astype(
        jnp.bfloat16
    )
    neigh_local = lax.dot_general(mean_rows, d_pre, over_rows, preferred_element_type=jnp.float32)
    self_local = lax.dot_general(features, d_pre, over_rows, preferred_element_type=jnp.float32)
    bias_local = jnp.sum(d_pre.astype(jnp.float32), axis=0)
    grad_w_neigh, grad_w_self, grad_bias = lax.psum(
        (neigh_local, self_local, bias_local), ("blk", "rep")
    )
    mean_own = lax.dot_general(d_pre, w_neigh, over_cols, preferred_element_type=jnp.float32)
    mean_own = (mean_own / divisor[:, None]).astype(jnp.bfloat16)
    mean_grad = lax.all_gather(mean_own, "blk", axis=0, tiled=True)
    mean_tiles = mean_grad.reshape(row_tiles, edge, width)

    def backward_block(start, block_size, partial_back):
        tile_block = lax.dynamic_slice_in_dim(tiles, start, block_size, 0)
        rows_here = lax.dynamic_slice_in_dim(row_index, start, block_size, 0)
        cols_here = lax.dynamic_slice_in_dim(col_index, start, block_size, 0)
        alive = (start + jnp.arange(block_size) < live_tiles).astype(jnp.float32)
        picked = mean_tiles[rows_here]
        products = jnp.einsum(
            "tij,tid->tjd", tile_block, picked, preferred_element_type=jnp.float32
        )
        return partial_back.at[cols_here].add(products * alive[:, None, None])

    back_part = tile_pass(tiles, backward_block, jnp.zeros((col_tiles, edge, width), jnp.float32))
    back_rounded = back_part.reshape(block_rows, width).astype(jnp.bfloat16).astype(jnp.float32)
    back = lax.psum_scatter(
        back_rounded.astype(jnp.bfloat16), "rep", scatter_dimension=0, tiled=True
    ).astype(jnp.float32)
    grad_features = lax.dot_general(d_pre, w_self, over_cols, preferred_element_type=jnp.float32)
    grad_features = (grad_features + back).astype(jnp.bfloat16)
    return (activations, grad_features, grad_w_neigh, grad_w_self, grad_bias)


def solution(mesh):
    in_specs = (
        P(("blk", "rep"), None),
        P("blk", "rep", None, None, None),
        P("blk", "rep", None),
        P("blk", "rep", None),
        P("blk", "rep"),
        P(),
        P(),
        P(),
        P(("blk", "rep"), None),
    )
    out_specs = (P(("blk", "rep"), None), P(("blk", "rep"), None), P(), P(), P())
    return jax.shard_map(local, mesh=mesh, in_specs=in_specs, out_specs=out_specs, check_vma=False)
```

profile of v0, /device:TPU:2, one launch (start us, length us, event | category | flops | bytes accessed | tf_op | source)
XLA Modules:
  0.0 803.5 jit_solution(6707782587209004010)
XLA Ops:
  8.0 41.5 %all-gather.3.cloned.1.call-done = bf16[8192,256]{1,0:T(8,128)(2,1)} async-done(((bf16[512,256]{1,0:T(8,128)(2,1)}), bf16[8192,256]{1,0:T(8,128)(2,1)}) %all-gather.3.cloned.1.call-update) | async-done | bytes 4194320 | tf_op jit(solution)/shard_map/all_gather | solution.py:33
  52.0 283.7 %while.28 = (s32[]{:T(128)}, f32[32,128,256]{2,1,0:T(8,128)}, f32[32,128]{1,0:T(8,128)S(1)}, s32[512]{0:T(512)S(1)}, bf16[512,128,128]{2,1,0:T(8,128)(2,1)}, /*i...) while((s32[]{:T(128)}, f32[32,128,256]{2,1,0:T(8,128)}, ...), condition=%wide.region_4.0_spmd, body=%wide.region_0.0_spmd.sunk | while | flops 543172160 | bytes 50420668 | solution.py:17
  65.0 19.4 %scatter_fusion = f32[32,128,256]{2,1,0:T(8,128)} fusion(f32[32,128,256]{2,1,0:T(8,128)} %get-tuple-element.450, s32[64]{0:T(128)S(1)} %get-tuple-element.426, f32[64,128,256]{2,1,0:T(8,128)} %broadcast_multiply_fusion.4), kind=kCustom, calls=%fused_computation.2.clone.1 | custom fusion | flops 2097152 | bytes 25166080 | tf_op jit(solution)/shard_map/while/body/eval_jaxpr/scatter-add | solution.py:46
  100.5 19.1 %scatter_fusion = f32[32,128,256]{2,1,0:T(8,128)} fusion(f32[32,128,256]{2,1,0:T(8,128)} %get-tuple-element.450, s32[64]{0:T(128)S(1)} %get-tuple-element.426, f32[64,128,256]{2,1,0:T(8,128)} %broadcast_multiply_fusion.4), kind=kCustom, calls=%fused_computation.2.clone.1 | custom fusion | flops 2097152 | bytes 25166080 | tf_op jit(solution)/shard_map/while/body/eval_jaxpr/scatter-add | solution.py:46
  135.8 19.2 %scatter_fusion = f32[32,128,256]{2,1,0:T(8,128)} fusion(f32[32,128,256]{2,1,0:T(8,128)} %get-tuple-element.450, s32[64]{0:T(128)S(1)} %get-tuple-element.426, f32[64,128,256]{2,1,0:T(8,128)} %broadcast_multiply_fusion.4), kind=kCustom, calls=%fused_computation.2.clone.1 | custom fusion | flops 2097152 | bytes 25166080 | tf_op jit(solution)/shard_map/while/body/eval_jaxpr/scatter-add | solution.py:46
  171.2 19.2 %scatter_fusion = f32[32,128,256]{2,1,0:T(8,128)} fusion(f32[32,128,256]{2,1,0:T(8,128)} %get-tuple-element.450, s32[64]{0:T(128)S(1)} %get-tuple-element.426, f32[64,128,256]{2,1,0:T(8,128)} %broadcast_multiply_fusion.4), kind=kCustom, calls=%fused_computation.2.clone.1 | custom fusion | flops 2097152 | bytes 25166080 | tf_op jit(solution)/shard_map/while/body/eval_jaxpr/scatter-add | solution.py:46
  206.6 19.2 %scatter_fusion = f32[32,128,256]{2,1,0:T(8,128)} fusion(f32[32,128,256]{2,1,0:T(8,128)} %get-tuple-element.450, s32[64]{0:T(128)S(1)} %get-tuple-element.426, f32[64,128,256]{2,1,0:T(8,128)} %broadcast_multiply_fusion.4), kind=kCustom, calls=%fused_computation.2.clone.1 | custom fusion | flops 2097152 | bytes 25166080 | tf_op jit(solution)/shard_map/while/body/eval_jaxpr/scatter-add | solution.py:46
  242.1 19.2 %scatter_fusion = f32[32,128,256]{2,1,0:T(8,128)} fusion(f32[32,128,256]{2,1,0:T(8,128)} %get-tuple-element.450, s32[64]{0:T(128)S(1)} %get-tuple-element.426, f32[64,128,256]{2,1,0:T(8,128)} %broadcast_multiply_fusion.4), kind=kCustom, calls=%fused_computation.2.clone.1 | custom fusion | flops 2097152 | bytes 25166080 | tf_op jit(solution)/shard_map/while/body/eval_jaxpr/scatter-add | solution.py:46
  277.5 19.5 %scatter_fusion = f32[32,128,256]{2,1,0:T(8,128)} fusion(f32[32,128,256]{2,1,0:T(8,128)} %get-tuple-element.450, s32[64]{0:T(128)S(1)} %get-tuple-element.426, f32[64,128,256]{2,1,0:T(8,128)} %broadcast_multiply_fusion.4), kind=kCustom, calls=%fused_computation.2.clone.1 | custom fusion | flops 2097152 | bytes 25166080 | tf_op jit(solution)/shard_map/while/body/eval_jaxpr/scatter-add | solution.py:46
  313.1 19.3 %scatter_fusion = f32[32,128,256]{2,1,0:T(8,128)} fusion(f32[32,128,256]{2,1,0:T(8,128)} %get-tuple-element.450, s32[64]{0:T(128)S(1)} %get-tuple-element.426, f32[64,128,256]{2,1,0:T(8,128)} %broadcast_multiply_fusion.4), kind=kCustom, calls=%fused_computation.2.clone.1 | custom fusion | flops 2097152 | bytes 25166080 | tf_op jit(solution)/shard_map/while/body/eval_jaxpr/scatter-add | solution.py:46
  341.0 41.3 %all-reduce = f32[4096]{0:T(1024)S(1)} all-reduce(f32[4096]{0:T(1024)S(1)} %bitcast.36), channel_id=3, replica_groups=mesh['blk'=8,'rep'=16] {'blk'}, use_global_device_ids=true, to_apply=%region_6.0.clone | all-reduce | flops 4096 | bytes 32768
  382.4 32.2 %reduce-scatter.3.cloned.1.call-done = bf16[512,256]{1,0:T(8,128)(2,1)} async-done(((bf16[4096,256]{1,0:T(8,128)(2,1)}), bf16[512,256]{1,0:T(8,128)(2,1)}) %reduce-scatter.3.cloned.1.call-update) | async-done | bytes 262160 | tf_op jit(solution)/shard_map/reduce_scatter | solution.py:58
  418.0 22.5 %copy.17 = bf16[1,1,512,128,128]{3,4,2,1,0:T(8,128)(2,1)} copy(bf16[1,1,512,128,128]{4,3,2,1,0:T(8,128)(2,1)} %bitcast.32) | data formatting | bytes 33554432 | tf_op args[1]
  442.6 28.2 %all-gather.5.cloned.1.call-done = bf16[4096,256]{1,0:T(8,128)(2,1)} async-done(((bf16[512,256]{1,0:T(8,128)(2,1)}), bf16[4096,256]{1,0:T(8,128)(2,1)}) %all-gather.5.cloned.1.call-update) | async-done | bytes 2097168 | tf_op jit(solution)/shard_map/all_gather | solution.py:80
  475.1 243.1 %while.29 = (s32[]{:T(128)}, f32[64,128,256]{2,1,0:T(8,128)}, s32[512]{0:T(512)S(1)}, bf16[512,128,128]{1,2,0:T(8,128)(2,1)}, s32[512]{0:T(512)S(1)}, /*index=5*...) while((s32[]{:T(128)}, f32[64,128,256]{2,1,0:T(8,128)}, ...), condition=%wide.region_9.10_spmd, body=%wide.region_7.0_spmd.sunk | while | flops 541066816 | bytes 48241072 | solution.py:17
  486.0 19.7 %scatter_fusion.1 = f32[64,128,256]{2,1,0:T(8,128)} fusion(f32[64,128,256]{2,1,0:T(8,128)} %get-tuple-element.485, s32[64]{0:T(128)S(1)} %get-tuple-element.435, f32[64,128,256]{2,1,0:T(8,128)} %broadcast_multiply_fusion.5), kind=kCustom, calls=%fused_computation.4.clone.1 | custom fusion | flops 2097152 | bytes 25166080 | tf_op jit(solution)/shard_map/while/body/eval_jaxpr/scatter-add | solution.py:92
  516.6 19.6 %scatter_fusion.1 = f32[64,128,256]{2,1,0:T(8,128)} fusion(f32[64,128,256]{2,1,0:T(8,128)} %get-tuple-element.485, s32[64]{0:T(128)S(1)} %get-tuple-element.435, f32[64,128,256]{2,1,0:T(8,128)} %broadcast_multiply_fusion.5), kind=kCustom, calls=%fused_computation.4.clone.1 | custom fusion | flops 2097152 | bytes 25166080 | tf_op jit(solution)/shard_map/while/body/eval_jaxpr/scatter-add | solution.py:92
  547.1 19.5 %scatter_fusion.1 = f32[64,128,256]{2,1,0:T(8,128)} fusion(f32[64,128,256]{2,1,0:T(8,128)} %get-tuple-element.485, s32[64]{0:T(128)S(1)} %get-tuple-element.435, f32[64,128,256]{2,1,0:T(8,128)} %broadcast_multiply_fusion.5), kind=kCustom, calls=%fused_computation.4.clone.1 | custom fusion | flops 2097152 | bytes 25166080 | tf_op jit(solution)/shard_map/while/body/eval_jaxpr/scatter-add | solution.py:92
  577.5 19.2 %scatter_fusion.1 = f32[64,128,256]{2,1,0:T(8,128)} fusion(f32[64,128,256]{2,1,0:T(8,128)} %get-tuple-element.485, s32[64]{0:T(128)S(1)} %get-tuple-element.435, f32[64,128,256]{2,1,0:T(8,128)} %broadcast_multiply_fusion.5), kind=kCustom, calls=%fused_computation.4.clone.1 | custom fusion | flops 2097152 | bytes 25166080 | tf_op jit(solution)/shard_map/while/body/eval_jaxpr/scatter-add | solution.py:92
  607.7 19.4 %scatter_fusion.1 = f32[64,128,256]{2,1,0:T(8,128)} fusion(f32[64,128,256]{2,1,0:T(8,128)} %get-tuple-element.485, s32[64]{0:T(128)S(1)} %get-tuple-element.435, f32[64,128,256]{2,1,0:T(8,128)} %broadcast_multiply_fusion.5), kind=kCustom, calls=%fused_computation.4.clone.1 | custom fusion | flops 2097152 | bytes 25166080 | tf_op jit(solution)/shard_map/while/body/eval_jaxpr/scatter-add | solution.py:92
  638.0 19.4 %scatter_fusion.1 = f32[64,128,256]{2,1,0:T(8,128)} fusion(f32[64,128,256]{2,1,0:T(8,128)} %get-tuple-element.485, s32[64]{0:T(128)S(1)} %get-tuple-element.435, f32[64,128,256]{2,1,0:T(8,128)} %broadcast_multiply_fusion.5), kind=kCustom, calls=%fused_computation.4.clone.1 | custom fusion | flops 2097152 | bytes 25166080 | tf_op jit(solution)/shard_map/while/body/eval_jaxpr/scatter-add | solution.py:92
  668.3 19.4 %scatter_fusion.1 = f32[64,128,256]{2,1,0:T(8,128)} fusion(f32[64,128,256]{2,1,0:T(8,128)} %get-tuple-element.485, s32[64]{0:T(128)S(1)} %get-tuple-element.435, f32[64,128,256]{2,1,0:T(8,128)} %broadcast_multiply_fusion.5), kind=kCustom, calls=%fused_computation.4.clone.1 | custom fusion | flops 2097152 | bytes 25166080 | tf_op jit(solution)/shard_map/while/body/eval_jaxpr/scatter-add | solution.py:92
  698.6 19.5 %scatter_fusion.1 = f32[64,128,256]{2,1,0:T(8,128)} fusion(f32[64,128,256]{2,1,0:T(8,128)} %get-tuple-element.485, s32[64]{0:T(128)S(1)} %get-tuple-element.435, f32[64,128,256]{2,1,0:T(8,128)} %broadcast_multiply_fusion.5), kind=kCustom, calls=%fused_computation.4.clone.1 | custom fusion | flops 2097152 | bytes 25166080 | tf_op jit(solution)/shard_map/while/body/eval_jaxpr/scatter-add | solution.py:92
  724.1 67.5 %psum.23 = f32[256]{0:T(256)} all-reduce(f32[256]{0:T(256)S(1)} %get-tuple-element.330), channel_id=1, replica_groups=mesh['blk'=8,'rep'=16] {'blk','rep'}, use_global_device_ids=true, to_apply=%region_14.15 | all-reduce | flops 256 | bytes 2048 | tf_op jit(solution)/shard_map/psum | solution.py:75
  (143 shorter events, 245.3 us)
Async XLA Ops:
  7.2 408.6 %copy-start = (bf16[256,256]{1,0:T(8,128)(2,1)S(1)}, bf16[256,256]{1,0:T(8,128)(2,1)}, u32[]{:S(2)}) copy-start(bf16[256,256]{1,0:T(8,128)(2,1)} %param.19) | copy-start | bytes 393220
  7.2 44.8 %copy-start.3 = (s32[1,1,512]{2,1,0:T(1,128)S(1)}, s32[1,1,512]{2,1,0:T(1,128)}, u32[]{:S(2)}) copy-start(s32[1,1,512]{2,1,0:T(1,128)} %param.15) | copy-start | bytes 6148
  7.2 44.8 %copy-start.4 = (s32[1,1,512]{2,1,0:T(1,128)S(1)}, s32[1,1,512]{2,1,0:T(1,128)}, u32[]{:S(2)}) copy-start(s32[1,1,512]{2,1,0:T(1,128)} %param.16) | copy-start | bytes 6148
  7.2 42.3 %all-gather.3.cloned.1.call-start = ((), (), s32[]{:S(2)}) async-start(), calls=%async_computation.2 | async-start | bytes 4456448 | tf_op jit(solution)/shard_map/all_gather | solution.py:33
  7.9 406.6 %reduce-scatter.3.cloned.1.call-start = ((), (), s32[]{:S(2)}) async-start(), calls=%async_computation.3 | async-start | bytes 2359296 | tf_op jit(solution)/shard_map/reduce_scatter | solution.py:58
  335.7 4.0 copy-start.9
  335.7 78.8 %copy-start.7 = (bf16[256,256]{1,0:T(8,128)(2,1)S(1)}, bf16[256,256]{1,0:T(8,128)(2,1)}, u32[]{:S(2)}) copy-start(bf16[256,256]{1,0:T(8,128)(2,1)} %param.18) | copy-start | bytes 393220
  335.7 80.1 %copy-start.2 = (bf16[512,256]{1,0:T(8,128)(2,1)S(1)}, bf16[512,256]{1,0:T(8,128)(2,1)}, u32[]{:S(2)}) copy-start(bf16[512,256]{1,0:T(8,128)(2,1)} %param.13) | copy-start | bytes 786436
  335.7 80.1 %copy-start.5 = (bf16[512,256]{1,0:T(8,128)(2,1)S(1)}, bf16[512,256]{1,0:T(8,128)(2,1)}, u32[]{:S(2)}) copy-start(bf16[512,256]{1,0:T(8,128)(2,1)} %param.21) | copy-start | bytes 786436
  335.7 80.1 %copy-start.8 = (f32[256]{0:T(256)S(1)}, f32[256]{0:T(256)}, u32[]{:S(2)}) copy-start(f32[256]{0:T(256)} %param.20) | copy-start | bytes 3076
  339.7 131.2 %all-gather.5.cloned.1.call-start = ((), (), s32[]{:S(2)}) async-start(), calls=%async_computation.4 | async-start | bytes 2359296 | tf_op jit(solution)/shard_map/all_gather | solution.py:80
  418.0 373.7 %all-reduce.4.cloned.1.call-start = ((), (), s32[]{:S(2)}) async-start(), calls=%async_computation.6 | async-start | bytes 1048576 | tf_op jit(solution)/shard_map/psum | solution.py:75
  418.0 23.5 %copy-start.6 = (bf16[512,256]{1,0:T(8,128)(2,1)S(1)}, bf16[512,256]{1,0:T(8,128)(2,1)}, u32[]{:S(2)}) copy-start(bf16[512,256]{1,0:T(8,128)(2,1)} %reduce-scatter.3.cloned.1.call-done) | copy-start | bytes 786436
  442.6 350.8 %reduce-scatter.5.cloned.1.call-start = ((), (), s32[]{:S(2)}) async-start(), calls=%async_computation.5 | async-start | bytes 4456448 | tf_op jit(solution)/shard_map/reduce_scatter | solution.py:96
  470.8 4.2 copy-start.1
Sparse Core Ops, SparseCore 0:
  9.7 39.7 all-gather.2
  339.8 74.7 reduce-scatter.2
  418.1 52.6 all-gather.4
  476.2 143.6 all-reduce.3
  724.2 65.9 reduce-scatter.4
where the time goes:
time: 807 us; the launch traced here: 804 us
  other arithmetic  357 us (44%)
  matrix products  124 us (15%)
  blocking collectives  109 us (14%)
  waiting for transfers between devices  103 us (13%)
  local copies, waits for them, and re-layouts  95.7 us (12%)
  between operations  14.6 us (2%)
    scatter-add x8, other arithmetic, backward_block(): return partial_back.at[cols_here].add(products * alive[:, None, None])  156 us
    scatter-add x8, other arithmetic, forward_block(): partial_value.at[rows_here].add(products * alive[:, None, None])  154 us
    psum x1, blocking collectives, local(): lax.psum((neigh_local, self_local, bias_local), ('blk', 'rep'))  67.5 us
    dot_general x8, matrix products, backward_block(): jnp.einsum('tij,tid->tjd', tile_block, picked, preferred_element_type=jnp...  58.3 us
    dot_general x8, matrix products, forward_block(): jnp.einsum('tij,tjd->tid', tile_block, picked, preferred_element_type=jnp...  58.3 us
    all_gather x1, waiting for transfers between devices, local(): lax.all_gather(features, 'rep', axis=0, tiled=True)  41.5 us
    unnamed x1, blocking collectives  41.3 us
    gather x8, local copies, waits for them, and re-layouts, forward_block(): picked = sources[cols_here]  39.6 us
  transfers between devices with their start and end apart: 5, of which 3 were waited for; matrix products, arithmetic and copies ran while one was open for 35% of the time, Pallas kernels for 0%

commit v1 on v0

v1 whole, which is shorter than its diff:
```python
import functools

import jax
import jax.numpy as jnp
from jax import lax
from jax.experimental import pallas as pl
from jax.experimental.pallas import tpu as pltpu
from jax.sharding import PartitionSpec as P

EDGE = 128
GROUP = 4
UNROLL = 8
AHEAD = 4
BODY = GROUP * UNROLL
OVER_ROWS = (((0,), (0,)), ((), ()))
OVER_COLS = (((1,), (1,)), ((), ()))


def body_count(slots, groups):
    steps = slots // GROUP + groups * (GROUP - 1) // GROUP
    return -(-steps // UNROLL)


def schedule(keys, others, live, groups):
    slots = keys.shape[0]
    places = body_count(slots, groups) * BODY
    index = jnp.arange(slots, dtype=jnp.int32)
    alive = index < live
    before = (keys[None, :] == keys[:, None]) & (index[None, :] < index[:, None])
    rank = jnp.sum(before.astype(jnp.int32), axis=1)
    ids = jnp.arange(groups, dtype=jnp.int32)
    counts = jnp.sum(((keys[None, :] == ids[:, None]) & alive[None, :]).astype(jnp.int32), axis=1)
    steps = (counts + GROUP - 1) // GROUP
    base = jnp.sum(jnp.where(ids[None, :] < keys[:, None], steps[None, :], 0), axis=1)
    place = jnp.where(alive, base * GROUP + rank, -1)
    hit = place[None, :] == jnp.arange(places, dtype=jnp.int32)[:, None]
    packed = (index * 64 + others) * 64 + keys + 1
    found = jnp.sum(jnp.where(hit, packed[None, :], 0), axis=1)
    code = jnp.maximum(found - 1, 0)
    slot = jnp.where(found > 0, code // 4096, slots)
    other = (code // 64) % 64
    key = (code % 64)[::GROUP]
    total = jnp.sum(steps).reshape(1)
    return slot, other, key, total


def tile_kernel(step, slot_ref, total_ref, tiles, zero_tile, buf, sems):
    slots = tiles.shape[0]
    bodies = lax.div(total_ref[0] + UNROLL - 1, UNROLL)

    def issue(body):
        def one(k, _):
            place = body * BODY + k
            slot = slot_ref[place]

            @pl.when(slot < slots)
            def _():
                pltpu.make_async_copy(tiles.at[slot], buf.at[place], sems.at[body]).start()

            @pl.when(slot >= slots)
            def _():
                pltpu.make_async_copy(zero_tile, buf.at[place], sems.at[body]).start()

            return 0

        lax.fori_loop(0, BODY, one, 0, unroll=4)

    for body in range(AHEAD):
        pl.when(body < bodies)(functools.partial(issue, body))

    @pl.loop(0, bodies)
    def _(body):
        pl.when(body + AHEAD < bodies)(lambda: issue(body + AHEAD))
        here = buf.at[pl.ds(body * BODY, BODY)]
        pltpu.make_async_copy(here, here, sems.at[body]).wait()
        for k in range(UNROLL):
            step(body * UNROLL + k)


def forward_kernel(
    slot_ref, other_ref, key_ref, total_ref, tiles, zero_tile, sources, out, degree, buf, acc, sems
):
    acc[...] = jnp.zeros_like(acc)
    degree[...] = jnp.zeros_like(degree)
    ones = jnp.ones((16, EDGE), jnp.bfloat16)

    def step(n):
        places = [n * GROUP + m for m in range(GROUP)]
        parts = [buf[p] for p in places]
        left = jnp.concatenate(parts, axis=1)
        right = jnp.concatenate([sources[other_ref[p]] for p in places], axis=0)
        row = key_ref[n]
        acc[row] += jnp.dot(left, right, preferred_element_type=jnp.float32)
        marks = (parts[0] + parts[1]) + (parts[2] + parts[3])
        degree[row] += lax.dot_general(ones, marks, OVER_COLS, preferred_element_type=jnp.float32)

    tile_kernel(step, slot_ref, total_ref, tiles, zero_tile, buf, sems)
    out[...] = acc[...].astype(out.dtype)


def backward_kernel(
    slot_ref, other_ref, key_ref, total_ref, tiles, zero_tile, grads, out, buf, acc, sems
):
    acc[...] = jnp.zeros_like(acc)

    def step(n):
        places = [n * GROUP + m for m in range(GROUP)]
        left = jnp.concatenate([grads[other_ref[p]] for p in places], axis=1)
        right = jnp.concatenate([buf[p] for p in places], axis=0)
        col = key_ref[n]
        acc[col] += jnp.dot(left, right, preferred_element_type=jnp.float32)

    tile_kernel(step, slot_ref, total_ref, tiles, zero_tile, buf, sems)
    out[...] = acc[...].astype(out.dtype)


def tile_call(kernel, sched, tiles, table, out_shape, acc_shape):
    slots = tiles.shape[0]
    bodies = body_count(slots, acc_shape[0])
    zero_tile = jnp.zeros((EDGE, EDGE), tiles.dtype)
    vmem = pl.BlockSpec(memory_space=pltpu.VMEM)
    smem = pl.BlockSpec(memory_space=pltpu.SMEM)
    hbm = pl.BlockSpec(memory_space=pl.ANY)
    return pl.pallas_call(
        kernel,
        out_shape=out_shape,
        in_specs=[smem] * 4 + [hbm, hbm, vmem],
        out_specs=jax.tree.map(lambda _: vmem, out_shape),
        scratch_shapes=[
            pltpu.VMEM((bodies * BODY, EDGE, EDGE), tiles.dtype),
            pltpu.VMEM(acc_shape, jnp.float32),
            pltpu.SemaphoreType.DMA((bodies,)),
        ],
        compiler_params=pltpu.CompilerParams(vmem_limit_bytes=56 << 20),
    )(*sched, tiles, zero_tile, table)


def local(features, adj_tiles, tile_rows, tile_cols, tile_count, w_neigh, w_self, bias, out_grad):
    tiles = adj_tiles[0, 0]
    row_index = tile_rows[0, 0]
    col_index = tile_cols[0, 0]
    live_tiles = tile_count[0, 0]
    span, width = features.shape
    n_blk, n_rep = lax.axis_size("blk"), lax.axis_size("rep")
    row_tiles = span * n_blk // EDGE
    col_tiles = span * n_rep // EDGE
    per_span = span // EDGE
    f32, bf16 = jnp.float32, jnp.bfloat16

    sources = lax.all_gather(features, "rep", axis=0, tiled=True).reshape(col_tiles, EDGE, width)
    forward_plan = schedule(row_index, col_index, live_tiles, row_tiles)
    backward_plan = schedule(col_index, row_index, live_tiles, col_tiles)
    partial, degree_part = tile_call(
        forward_kernel,
        forward_plan,
        tiles,
        sources,
        (
            jax.ShapeDtypeStruct((row_tiles, EDGE, width), bf16),
            jax.ShapeDtypeStruct((row_tiles, 16, EDGE), f32),
        ),
        (row_tiles, EDGE, width),
    )
    aggregate = lax.psum_scatter(
        partial.reshape(row_tiles * EDGE, width), "blk", scatter_dimension=0, tiled=True
    ).astype(f32)
    degree = lax.psum_scatter(
        degree_part[:, 0].reshape(row_tiles * EDGE), "blk", scatter_dimension=0, tiled=True
    )
    divisor = jnp.maximum(degree, 1.0)
    mean_rows = (aggregate / divisor[:, None]).astype(bf16)
    pre = jnp.dot(mean_rows, w_neigh, preferred_element_type=f32)
    pre = pre + jnp.dot(features, w_self, preferred_element_type=f32) + bias
    activations = jax.nn.silu(pre).astype(bf16)
    sigma = jax.nn.sigmoid(pre)
    d_pre = (out_grad.astype(f32) * sigma * (1.0 + pre * (1.0 - sigma))).astype(bf16)
    neigh_local = lax.dot_general(mean_rows, d_pre, OVER_ROWS, preferred_element_type=f32)
    self_local = lax.dot_general(features, d_pre, OVER_ROWS, preferred_element_type=f32)
    bias_local = jnp.sum(d_pre.astype(f32), axis=0)
    grad_w_neigh, grad_w_self, grad_bias = lax.psum(
        (neigh_local, self_local, bias_local), ("blk", "rep")
    )
    mean_own = lax.dot_general(w_neigh, d_pre, OVER_COLS, preferred_element_type=f32)
    mean_own = (mean_own / divisor[None, :]).astype(bf16)
    mean_own = mean_own.reshape(width, per_span, EDGE).transpose(1, 0, 2)
    grads = lax.all_gather(mean_own, "blk", axis=0, tiled=True)
    back_part = tile_call(
        backward_kernel,
        backward_plan,
        tiles,
        grads,
        jax.ShapeDtypeStruct((col_tiles, width, EDGE), bf16),
        (col_tiles, width, EDGE),
    )
    back = lax.psum_scatter(back_part, "rep", scatter_dimension=0, tiled=True)
    back = back.transpose(0, 2, 1).reshape(span, width).astype(f32)
    grad_features = lax.dot_general(d_pre, w_self, OVER_COLS, preferred_element_type=f32)
    grad_features = (grad_features + back).astype(bf16)
    return (activations, grad_features, grad_w_neigh, grad_w_self, grad_bias)


def solution(mesh):
    spans = P(("blk", "rep"), None)
    in_specs = (
        spans,
        P("blk", "rep", None, None, None),
        P("blk", "rep", None),
        P("blk", "rep", None),
        P("blk", "rep"),
        P(),
        P(),
        P(),
        spans,
    )
    out_specs = (spans, spans, P(), P(), P())
    return jax.shard_map(local, mesh=mesh, in_specs=in_specs, out_specs=out_specs, check_vma=False)
```

time: 807 us -> 427 us (0.53)
  other arithmetic: 357 us -> 9.89 us
  waiting for transfers between devices: 103 us -> 245 us
  matrix products: 124 us -> 5.65 us
  local copies, waits for them, and re-layouts: 95.7 us -> 7.74 us
  Pallas kernels: 0 us -> 25.1 us
    scatter-add x24 -> x0, other arithmetic: 318 us -> none  [the longest x8 156 us: backward_block(): return partial_back.at[cols_here].add(products * alive[:, None, None])]
    dot_general x22 -> x6, matrix products: 124 us -> 5.65 us  [the longest x1 1.22 us: local(): pre = jnp.dot(mean_rows, w_neigh, preferred_element_type=f32)]
    reduce_scatter x2, waiting for transfers between devices: 32.2 us -> 99.9 us  [the longest x1 66.1 us: local(): back = lax.psum_scatter(back_part, 'rep', scatter_dimension=0, tiled=True)]
    psum x1, waiting for transfers between devices: 0.01 us -> 62.7 us  [local(): lax.psum((neigh_local, self_local, bias_local), ('blk', 'rep'))]
    gather x16 -> x0, local copies, waits for them, and re-layouts: 62.5 us -> none  [the longest x8 39.6 us: forward_block(): picked = sources[cols_here]]
    pallas_call x0 -> x2, Pallas kernels: none -> 25.1 us  [tile_call(): pl.pallas_call(kernel, out_shape=out_shape, in_specs=[smem] * 4 + [hbm, h...]
    unnamed x24 -> x19, local copies, waits for them, and re-layouts: 26.6 us -> 3.64 us
    all_gather x1, waiting for transfers between devices: 28.2 us -> 49.1 us  [local(): grads = lax.all_gather(mean_own, 'blk', axis=0, tiled=True)]
  transfers between devices with their start and end apart: 5 -> 5, of which waited for: 3 -> 5; matrix products, arithmetic and copies ran while one was open for 35% -> 4% of each run, Pallas kernels for 0% -> 3%
where the time goes in v1:
time: 427 us; the launch traced here: 425 us
  waiting for transfers between devices  245 us (57%)
  blocking collectives  117 us (27%)
  Pallas kernels  25.1 us (6%)
  between operations  15.2 us (4%)
  other arithmetic  9.89 us (2%)
  local copies, waits for them, and re-layouts  7.74 us (2%)
  matrix products  5.65 us (1%)
    psum x1, blocking collectives, local(): lax.psum((neigh_local, self_local, bias_local), ('blk', 'rep'))  72.8 us
    reduce_scatter x1, waiting for transfers between devices, local(): back = lax.psum_scatter(back_part, 'rep', scatter_dimension=0, tiled=True)  66.1 us
    psum x1, waiting for transfers between devices, local(): lax.psum((neigh_local, self_local, bias_local), ('blk', 'rep'))  62.7 us
    all_gather x1, waiting for transfers between devices, local(): grads = lax.all_gather(mean_own, 'blk', axis=0, tiled=True)  49.1 us
    unnamed x1, blocking collectives  43.9 us
    reduce_scatter x1, waiting for transfers between devices, local(): lax.psum_scatter(partial.reshape(row_tiles * EDGE, width), 'blk', scatter...  33.8 us
    all_gather x1, waiting for transfers between devices, local(): lax.all_gather(features, 'rep', axis=0, tiled=True)  32.1 us
    pallas_call x2, Pallas kernels, tile_call(): pl.pallas_call(kernel, out_shape=out_shape, in_specs=[smem] * 4 + [hbm, h...  25.1 us
  transfers between devices with their start and end apart: 5, of which 5 were waited for; matrix products, arithmetic and copies ran while one was open for 4% of the time, Pallas kernels for 3%

profile of v1, /device:TPU:2, one launch (start us, length us, event | category | flops | bytes accessed | tf_op | source)
XLA Modules:
  0.0 425.0 jit_solution(12992952612416623430)
XLA Ops:
  8.6 0.8 convert_reduce_fusion.4
  10.8 0.8 convert_reduce_fusion.3
  12.3 0.8 select_reduce_fusion.2
  13.1 1.0 convert_reduce_fusion
  14.1 1.0 convert_reduce_fusion.1
  16.6 0.8 slice.9.key_ref
  17.4 32.1 %all-gather.3.cloned.1.call-done = bf16[8192,256]{1,0:T(8,128)(2,1)} async-done(((bf16[512,256]{1,0:T(8,128)(2,1)}), bf16[8192,256]{1,0:T(8,128)(2,1)}) %all-gather.3.cloned.1.call-update) | async-done | bytes 4194320 | tf_op jit(solution)/shard_map/all_gather | solution.py:150
  50.1 11.6 %shard_map.128 = (bf16[32,128,256]{2,1,0:T(8,128)(2,1)}, f32[32,16,128]{2,1,0:T(8,128)}) custom-call(s32[608]{0:T(1024)} %get-tuple-element.45.slot_ref, s32[608]{0:T(1024)} %get-tuple-element.44.other_ref, s32[152]{0:T(256)} %slice.9.key_ref, s32[1]{0:T(128)} %bitcast.3.total_ref, bf16[512,128,128]{2,1,0:T(8,128)(2,1)} %bitcast.32, ...), custom_call_target="tpu_custom_call" | custom-call | tf_op jit(solution)/shard_map/pallas_call | solution.py:124
  63.6 0.9 slice.10
  64.5 43.9 %all-reduce = f32[4096]{0:T(1024)S(1)} all-reduce(f32[4096]{0:T(1024)S(1)} %bitcast.38), channel_id=3, replica_groups=mesh['blk'=8,'rep'=16] {'blk'}, use_global_device_ids=true, to_apply=%region_6.7.clone | all-reduce | flops 4096 | bytes 32768
  108.4 33.8 %reduce-scatter.3.cloned.1.call-done = bf16[512,256]{1,0:T(8,128)(2,1)} async-done(((bf16[4096,256]{1,0:T(8,128)(2,1)}), bf16[512,256]{1,0:T(8,128)(2,1)}) %reduce-scatter.3.cloned.1.call-update) | async-done | bytes 262160 | tf_op jit(solution)/shard_map/reduce_scatter | solution.py:164
  142.3 1.2 fusion.14
  143.5 1.1 convert_reduce_fusion.2
  144.9 0.8 copy.21
  145.9 1.0 convolution_bitcast_fusion
  146.8 1.1 fusion.13
  149.6 49.1 %all-gather.5.cloned.1.call-done.grads = bf16[32,256,128]{2,1,0:T(8,128)(2,1)} async-done(((bf16[4,256,128]{2,1,0:T(8,128)(2,1)}), bf16[32,256,128]{2,1,0:T(8,128)(2,1)}) %all-gather.5.cloned.1.call-update) | async-done | bytes 2097168 | tf_op jit(solution)/shard_map/all_gather | solution.py:186
  198.7 13.6 %shard_map.129 = bf16[64,256,128]{2,1,0:T(8,128)(2,1)} custom-call(s32[704]{0:T(1024)} %get-tuple-element.40.slot_ref, s32[704]{0:T(1024)} %get-tuple-element.39.other_ref, s32[176]{0:T(256)} %slice.11.key_ref, s32[1]{0:T(128)} %bitcast.8.total_ref, bf16[512,128,128]{2,1,0:T(8,128)(2,1)} %bitcast.33, bf16[128,128]{1,0:T(8,128)(2,1)} %broadcast_14_zero_tile.2.zero_tile, ...), custom_call_target="tpu_custom_call" | custom-call | tf_op jit(solution)/shard_map/pallas_call | solution.py:124
  212.3 72.8 %psum.23 = f32[256]{0:T(256)} all-reduce(f32[256]{0:T(256)S(1)} %get-tuple-element.31), channel_id=1, replica_groups=mesh['blk'=8,'rep'=16] {'blk','rep'}, use_global_device_ids=true, to_apply=%region_16.17 | all-reduce | flops 256 | bytes 2048 | tf_op jit(solution)/shard_map/psum | solution.py:180
  285.1 62.7 %all-reduce.4.cloned.1.call-done = (f32[256,256]{1,0:T(8,128)}, f32[256,256]{0,1:T(8,128)}) async-done(((f32[256,256]{1,0:T(8,128)}, f32[256,256]{0,1:T(8,128)}), (f32[256,256]{1,0:T(8,128)}, f32[256,256]{0,1:T(8,128)})) %all-reduce.4.cloned.1.call-update) | async-done | bytes 524304 | tf_op jit(solution)/shard_map/psum | solution.py:180
  347.7 1.8 copy.23
  349.5 66.1 %reduce-scatter.5.cloned.1.call-done = bf16[4,256,128]{2,1,0:T(8,128)(2,1)} async-done(((bf16[64,256,128]{2,1,0:T(8,128)(2,1)}), bf16[4,256,128]{2,1,0:T(8,128)(2,1)}) %reduce-scatter.5.cloned.1.call-update) | async-done | bytes 262160 | tf_op jit(solution)/shard_map/reduce_scatter | solution.py:195
  415.6 1.0 convert_bitcast_fusion
  416.8 1.0 fusion.1
  (43 shorter events, 9.2 us)
Async XLA Ops:
  7.2 136.3 %copy-start = (bf16[256,256]{1,0:T(8,128)(2,1)S(1)}, bf16[256,256]{1,0:T(8,128)(2,1)}, u32[]{:S(2)}) copy-start(bf16[256,256]{1,0:T(8,128)(2,1)} %param.15) | copy-start | bytes 393220
  7.2 42.3 %all-gather.3.cloned.1.call-start = ((), (), s32[]{:S(2)}) async-start(), calls=%async_computation.2 | async-start | bytes 4456448 | tf_op jit(solution)/shard_map/all_gather | solution.py:150
  7.9 134.3 %reduce-scatter.3.cloned.1.call-start = ((), (), s32[]{:S(2)}) async-start(), calls=%async_computation.3 | async-start | bytes 2359296 | tf_op jit(solution)/shard_map/reduce_scatter | solution.py:164
  61.7 0.7 copy-start.7
  61.7 80.6 %copy-start.5 = (bf16[256,256]{1,0:T(8,128)(2,1)S(1)}, bf16[256,256]{1,0:T(8,128)(2,1)}, u32[]{:S(2)}) copy-start(bf16[256,256]{1,0:T(8,128)(2,1)} %param.14) | copy-start | bytes 393220
  61.7 81.8 %copy-start.1 = (bf16[512,256]{1,0:T(8,128)(2,1)S(1)}, bf16[512,256]{1,0:T(8,128)(2,1)}, u32[]{:S(2)}) copy-start(bf16[512,256]{1,0:T(8,128)(2,1)} %param.9) | copy-start | bytes 786436
  61.7 81.8 %copy-start.3 = (bf16[512,256]{1,0:T(8,128)(2,1)S(1)}, bf16[512,256]{1,0:T(8,128)(2,1)}, u32[]{:S(2)}) copy-start(bf16[512,256]{1,0:T(8,128)(2,1)} %param.17) | copy-start | bytes 786436
  61.8 81.8 %copy-start.6 = (f32[256]{0:T(256)S(1)}, f32[256]{0:T(256)}, u32[]{:S(2)}) copy-start(f32[256]{0:T(256)} %param.16) | copy-start | bytes 3076
  61.8 136.9 %all-gather.5.cloned.1.call-start = ((), (), s32[]{:S(2)}) async-start(), calls=%async_computation.4 | async-start | bytes 2359296 | tf_op jit(solution)/shard_map/all_gather | solution.py:186
  144.7 2.2 copy-start.4
  145.8 201.9 %all-reduce.4.cloned.1.call-start = ((), (), s32[]{:S(2)}) async-start(), calls=%async_computation.6 | async-start | bytes 1048576 | tf_op jit(solution)/shard_map/psum | solution.py:180
  147.9 267.7 %reduce-scatter.5.cloned.1.call-start = ((), (), s32[]{:S(2)}) async-start(), calls=%async_computation.5 | async-start | bytes 4456448 | tf_op jit(solution)/shard_map/reduce_scatter | solution.py:195
  349.5 68.3 %copy-start.2 = (f32[256,256]{1,0:T(8,128)S(1)}, f32[256,256]{1,0:T(8,128)}, u32[]{:S(2)}) copy-start(f32[256,256]{1,0:T(8,128)} %get-tuple-element.50) | copy-start | bytes 786436
Sparse Core Ops, SparseCore 0:
  9.7 39.7 all-gather.2
  61.8 80.3 reduce-scatter.2
  145.9 52.6 all-gather.4
  204.0 143.6 all-reduce.3
  350.1 65.4 reduce-scatter.4

commit v2 on v1

--- a/solution.py
+++ b/solution.py
@@ -7,6 +7,7 @@
 from jax.experimental.pallas import tpu as pltpu
 from jax.sharding import PartitionSpec as P
 
+MESH = pl.DeviceIdType.MESH
 EDGE = 128
 GROUP = 4
 UNROLL = 8
@@ -135,6 +136,371 @@
     )(*sched, tiles, zero_tile, table)
 
 
+def place_of():
+    blk, rep = lax.axis_index("blk"), lax.axis_index("rep")
+    y, x, z, core = blk // 2, (blk % 2) * 2 + rep // 8, (rep // 2) % 4, rep % 2
+
+    def device(dy=0, dx=0, dz=0, sibling=False, x_lo=False):
+        to_y, to_z = (y + dy) % 4, (z + dz) % 4
+        to_x = x + 1 - 2 * (x % 2) if x_lo else (x + dx) % 4
+        to_core = 1 - core if sibling else core
+        return (to_y * 2 + to_x // 2, (to_x % 2) * 8 + to_z * 2 + to_core)
+
+    return y, x, z, core, device
+
+
+def greet(devices):
+    barrier = pltpu.get_barrier_semaphore()
+    for device in devices:
+        pl.semaphore_signal(barrier, inc=1, device_id=device, device_id_type=MESH)
+    pl.semaphore_wait(barrier, len(devices))
+
+
+class Links:
+    def __init__(self, send_sems, recv_sems):
+        self.send_sems, self.recv_sems, self.sent = send_sems, recv_sems, []
+
+    def send(self, k, source, target, device):
+        copy = pltpu.make_async_remote_copy(
+            src_ref=source,
+            dst_ref=target,
+            send_sem=self.send_sems.at[k],
+            recv_sem=self.recv_sems.at[k],
+            device_id=device,
+            device_id_type=MESH,
+        )
+        copy.start()
+        self.sent.append(copy)
+
+    def arrived(self, k, target):
+        pltpu.make_async_copy(target, target, self.recv_sems.at[k]).wait()
+
+    def drain(self):
+        for copy in self.sent:
+            copy.wait_send()
+
+
+def gather_kernel(own, out, send_sems, recv_sems, own_sem):
+    y, x, z, core, device = place_of()
+    up, down, across, sibling = device(dz=1), device(dz=-1), device(x_lo=True), device(sibling=True)
+    links = Links(send_sems, recv_sems)
+    x_lo = x % 2
+
+    def block(dx, dz):
+        return ((x_lo + dx) % 2) * 8 + ((z + dz) % 4) * 2 + core
+
+    greet([up, down, across, sibling])
+    here = block(0, 0)
+    mine = pltpu.make_async_copy(own, out.at[here], own_sem)
+    mine.start()
+    for k, half, where in ((0, 0, up), (1, 1, down), (2, 0, across), (3, 1, across), (4, 1, up), (5, 0, down)):
+        links.send(k, own.at[half], out.at[here, half], where)
+    for half in range(2):
+        links.send(14 + half, own.at[half], out.at[here, half], sibling)
+    steps = (
+        (0, -1, 0, 0, (6, up)),
+        (1, 1, 0, 1, (7, down)),
+        (2, 0, 1, 0, (8, up)),
+        (3, 0, 1, 1, (9, down)),
+        (4, -1, 0, 1, (10, across)),
+        (5, 1, 0, 0, (11, across)),
+        (6, 2, 0, 0, None),
+        (7, 2, 0, 1, None),
+        (8, -1, 1, 0, (12, up)),
+        (9, 1, 1, 1, (13, down)),
+        (10, -1, 1, 1, None),
+        (11, 1, 1, 0, None),
+        (12, 2, 1, 0, None),
+        (13, 2, 1, 1, None),
+    )
+    for k, dz, dx, half, onward in steps:
+        piece = out.at[block(dx, dz), half]
+        links.arrived(k, piece)
+        if onward is not None:
+            links.send(onward[0], piece, piece, onward[1])
+        links.send(16 + k, piece, piece, sibling)
+    for half in range(2):
+        links.arrived(14 + half, out.at[here + 1 - 2 * core, half])
+    for k, dz, dx, half, _ in steps:
+        links.arrived(16 + k, out.at[block(dx, dz) + 1 - 2 * core, half])
+    mine.wait()
+    links.drain()
+
+
+def middle_kernel(
+    partial, degree, features, out_grad, w_neigh, w_self, bias,
+    act, grads, self_term, weight_grads, bias_grad,
+    from_y, sums, to_x, relay, from_x, degrees, mean, d_pre, own_grads, relay_grads,
+    rep_out, rep_in, blk_out, blk_in, send_sems, recv_sems, own_sem,
+):
+    f32, bf16 = jnp.float32, jnp.bfloat16
+    y, x, z, core, device = place_of()
+    blk, rep = lax.axis_index("blk"), lax.axis_index("rep")
+    n_blk, n_rep = 8, 16
+    x_hi = x // 2
+    links = Links(send_sems, recv_sems)
+    y_up, y_down, x_up, x_down = device(dy=1), device(dy=-1), device(dx=1), device(dx=-1)
+    blk_peer = lambda d: ((blk + d) % n_blk, rep)
+    rep_peer = lambda d: (blk, (rep + d) % n_rep)
+    greet([x_up, x_down] + [blk_peer(d) for d in range(1, n_blk)] + [rep_peer(d) for d in range(1, n_rep)])
+
+    def block(dy, j):
+        return ((y + dy) % 4) * 2 + (x_hi if j else 1 - x_hi)
+
+    def part(dy, j, half):
+        return partial.at[pl.ds(block(dy, j) * 4 + 2 * half, 2)]
+
+    def wide(ref):
+        return ref[...].astype(f32)
+
+    for d in range(1, n_blk):
+        to = (blk + d) % n_blk
+        links.send(D_DEGREE + d, degree.at[pl.ds(to * 4, 4)], degrees.at[d], blk_peer(d))
+
+    def raw_far(j):
+        links.send(D_Y + 6 * j, part(2, j, 0), from_y.at[j, 0], y_up)
+        links.send(D_Y + 6 * j + 1, part(2, j, 1), from_y.at[j, 1], y_down)
+
+    def raw_near(j):
+        links.send(D_Y + 6 * j + 2, part(1, j, 1), from_y.at[j, 2], y_up)
+        links.send(D_Y + 6 * j + 3, part(-1, j, 0), from_y.at[j, 3], y_down)
+
+    def combine(j):
+        for half, dy, y_to in ((0, 1, y_up), (1, -1, y_down)):
+            links.arrived(D_Y + 6 * j + half, from_y.at[j, half])
+            sums[j, half] = (wide(from_y.at[j, half]) + wide(part(dy, j, half))).astype(bf16)
+            links.send(D_Y + 6 * j + 4 + half, sums.at[j, half], from_y.at[j, 4 + half], y_to)
+
+    raw_far(0)
+    raw_near(0)
+    raw_far(1)
+    combine(0)
+    raw_near(1)
+    combine(1)
+    for j in range(2):
+        for slot in range(2, 6):
+            links.arrived(D_Y + 6 * j + slot, from_y.at[j, slot])
+        first = lambda j=j: wide(part(0, j, 0)) + wide(from_y.at[j, 3]) + wide(from_y.at[j, 4])
+        second = lambda j=j: wide(part(0, j, 1)) + wide(from_y.at[j, 2]) + wide(from_y.at[j, 5])
+        if j == 0:
+            to_x[0] = first().astype(bf16)
+            links.send(D_X, to_x.at[0], relay.at[0], x_up)
+            to_x[1] = second().astype(bf16)
+            links.send(D_X + 1, to_x.at[1], relay.at[1], x_down)
+            links.arrived(D_X, relay.at[0])
+            links.send(D_X + 2, relay.at[0], from_x.at[0], x_up)
+            links.arrived(D_X + 1, relay.at[1])
+            links.send(D_X + 3, relay.at[1], from_x.at[1], x_down)
+    for d in range(1, n_blk):
+        links.arrived(D_DEGREE + d, degrees.at[d])
+    total = degree[pl.ds(blk * 4, 4)]
+    for d in range(1, n_blk):
+        total += degrees[d]
+    divisor = jnp.maximum(total, 1.0)
+
+    def grads_at(dy, j, half):
+        return grads.at[pl.ds(block(dy, j) * 4 + 2 * half, 2)]
+
+    local_copies = []
+    for half, k, summed in ((0, D_X + 2, first), (1, D_X + 3, second)):
+        links.arrived(k, from_x.at[half])
+        aggregate = summed() + wide(from_x.at[half])
+        for t in (2 * half, 2 * half + 1):
+            rows = pl.ds(t * EDGE, EDGE)
+            lanes = divisor[t, 0:1]
+            down = jnp.transpose(jnp.broadcast_to(lanes, (EDGE, EDGE)))
+            down = jnp.concatenate([down, down], axis=1)
+            mean_rows = (aggregate[t - 2 * half] / down).astype(bf16)
+            pre = jnp.dot(mean_rows, w_neigh[...], preferred_element_type=f32)
+            pre = pre + jnp.dot(features[rows], w_self[...], preferred_element_type=f32) + bias[...]
+            sigma = jax.nn.sigmoid(pre)
+            act[rows] = (pre * sigma).astype(bf16)
+            here = (out_grad[rows].astype(f32) * sigma * (1.0 + pre * (1.0 - sigma))).astype(bf16)
+            mean[rows] = mean_rows
+            d_pre[rows] = here
+            back = lax.dot_general(w_neigh[...], here, OVER_COLS, preferred_element_type=f32)
+            own_grads[t] = (back / lanes).astype(bf16)
+        mine = own_grads.at[pl.ds(2 * half, 2)]
+        x_to, y_first, y_second = (x_up, y_up, y_down) if half == 0 else (x_down, y_down, y_up)
+        links.send(D_GX + half, mine, relay_grads.at[half], x_to)
+        links.send(D_GY + half, mine, grads_at(0, 1, half), y_first)
+        links.send(D_GY + 2 + half, mine, grads_at(0, 1, half), y_second)
+        copy = pltpu.make_async_copy(mine, grads_at(0, 1, half), own_sem.at[half])
+        copy.start()
+        local_copies.append(copy)
+
+    neigh = lax.dot_general(mean[...], d_pre[...], OVER_ROWS, preferred_element_type=f32)
+    own = lax.dot_general(features[...], d_pre[...], OVER_ROWS, preferred_element_type=f32)
+    column_sums = jnp.sum(d_pre[...].astype(f32), axis=0, keepdims=True)
+    high = column_sums.astype(bf16)
+    low = (column_sums - high.astype(f32)).astype(bf16)
+    which = lax.broadcasted_iota(jnp.int32, (16, 256), 0)
+    two_rows = jnp.where(which == 0, high.astype(f32), jnp.where(which == 1, low.astype(f32), 0.0)).astype(bf16)
+    for p in range(n_rep):
+        source = neigh if p < 8 else own
+        q = p % 8
+        rep_out[p, 0:32] = source[32 * q : 32 * q + 32].astype(bf16)
+        rep_out[p, 32:48] = two_rows
+    for d in range(1, n_rep):
+        links.send(D_REP + d, rep_out.at[(rep + d) % n_rep], rep_in.at[d], rep_peer(d))
+
+    other = ((x + 1) % 4) // 2
+    for half, x_to, there in ((0, x_up, (x + 3) % 4 // 2), (1, x_down, other)):
+        links.arrived(D_GX + half, relay_grads.at[half])
+        target = grads.at[pl.ds((y * 2 + there) * 4 + 2 * half, 2)]
+        links.send(D_GX + 2 + half, relay_grads.at[half], target, x_to)
+    links.arrived(D_GY, grads_at(-1, 1, 0))
+    links.send(D_GY + 4, grads_at(-1, 1, 0), grads_at(-1, 1, 0), y_up)
+    links.arrived(D_GY + 1, grads_at(1, 1, 1))
+    links.send(D_GY + 5, grads_at(1, 1, 1), grads_at(1, 1, 1), y_down)
+
+    self_term[...] = lax.dot_general(d_pre[...], w_self[...], OVER_COLS, preferred_element_type=f32)
+
+    rep_in[0] = rep_out[rep]
+    for d in range(1, n_rep):
+        links.arrived(D_REP + d, rep_in.at[d])
+    summed = rep_in[rep].astype(f32)
+    for source in range(1, n_rep):
+        summed += rep_in[(rep + n_rep - source) % n_rep].astype(f32)
+    kept = summed[0:32].astype(bf16)
+    column_sums = summed[32:33] + summed[33:34]
+    high = column_sums.astype(bf16)
+    low = (column_sums - high.astype(f32)).astype(bf16)
+    blk_out[0:32] = kept
+    blk_out[32:48] = jnp.where(which == 0, high.astype(f32), jnp.where(which == 1, low.astype(f32), 0.0)).astype(bf16)
+    for d in range(1, n_blk):
+        links.send(D_BLK + d, blk_out, blk_in.at[d], blk_peer(d))
+    blk_in[0] = blk_out[...]
+
+    links.arrived(D_GX + 2, grads_at(0, 0, 0))
+    links.send(D_GY + 6, grads_at(0, 0, 0), grads_at(0, 0, 0), y_up)
+    links.send(D_GY + 8, grads_at(0, 0, 0), grads_at(0, 0, 0), y_down)
+    links.arrived(D_GX + 3, grads_at(0, 0, 1))
+    links.send(D_GY + 7, grads_at(0, 0, 1), grads_at(0, 0, 1), y_down)
+    links.send(D_GY + 9, grads_at(0, 0, 1), grads_at(0, 0, 1), y_up)
+
+    for d in range(1, n_blk):
+        links.arrived(D_BLK + d, blk_in.at[d])
+    summed = blk_in[blk % n_blk].astype(f32)
+    for source in range(1, n_blk):
+        summed += blk_in[(blk + n_blk - source) % n_blk].astype(f32)
+    weight_grads[rep] = summed[0:32]
+    bias_grad[...] = jnp.broadcast_to(summed[32:33] + summed[33:34], bias_grad.shape)
+    for d in range(1, n_rep):
+        links.send(D_OUT + d, weight_grads.at[rep], weight_grads.at[rep], rep_peer(d))
+
+    links.arrived(D_GY + 6, grads_at(-1, 0, 0))
+    links.send(D_GY + 10, grads_at(-1, 0, 0), grads_at(-1, 0, 0), y_up)
+    links.arrived(D_GY + 7, grads_at(1, 0, 1))
+    links.send(D_GY + 11, grads_at(1, 0, 1), grads_at(1, 0, 1), y_down)
+    for j, base in ((1, D_GY), (0, D_GY + 6)):
+        links.arrived(base + 2, grads_at(1, j, 0))
+        links.arrived(base + 3, grads_at(-1, j, 1))
+        links.arrived(base + 4, grads_at(2, j, 0))
+        links.arrived(base + 5, grads_at(2, j, 1))
+    for d in range(1, n_rep):
+        links.arrived(D_OUT + d, weight_grads.at[(rep + n_rep - d) % n_rep])
+    for copy in local_copies:
+        copy.wait()
+    links.drain()
+
+
+D_DEGREE, D_Y, D_X, D_GX, D_GY, D_REP, D_BLK, D_OUT, D_ALL = 0, 8, 20, 24, 28, 40, 56, 64, 80
+
+
+def scatter_kernel(back, self_term, out, paired, arrivals, send_sems, recv_sems):
+    f32, bf16 = jnp.float32, jnp.bfloat16
+    y, x, z, core, device = place_of()
+    up, down, across, sibling = device(dz=1), device(dz=-1), device(x_lo=True), device(sibling=True)
+    links = Links(send_sems, recv_sems)
+    x_lo = x % 2
+    greet([up, down, across, sibling])
+    order = ((1, 2), (1, 1), (1, -1), (0, 2), (0, 1), (0, -1), (1, 0), (0, 0))
+
+    def block(dx, dz):
+        return ((x_lo + dx) % 2) * 8 + ((z + dz) % 4) * 2
+
+    for n, (dx, dz) in enumerate(order):
+        theirs = back.at[pl.ds((block(dx, dz) + 1 - core) * 4, 4)]
+        links.send(14 + n, theirs, paired.at[n], sibling)
+
+    def pair(dx, dz):
+        n = order.index((dx, dz))
+        links.arrived(14 + n, paired.at[n])
+        mine = back[pl.ds((block(dx, dz) + core) * 4, 4)]
+        paired[n] = (paired[n].astype(f32) + mine.astype(f32)).astype(bf16)
+
+    def piece(dx, dz, half):
+        return paired.at[order.index((dx, dz)), pl.ds(2 * half, 2)]
+
+    def send(k, dx, dz, half, where):
+        links.send(k, piece(dx, dz, half), arrivals.at[k], where)
+
+    def add(k, dx, dz, half):
+        links.arrived(k, arrivals.at[k])
+        ref = piece(dx, dz, half)
+        ref[...] = (ref[...].astype(f32) + arrivals[k].astype(f32)).astype(bf16)
+
+    pair(1, 2)
+    send(0, 1, 2, 0, down)
+    send(1, 1, 2, 1, up)
+    pair(1, 1)
+    send(2, 1, 1, 0, across)
+    pair(1, -1)
+    send(3, 1, -1, 1, across)
+    pair(0, 2)
+    send(4, 0, 2, 0, down)
+    send(5, 0, 2, 1, up)
+    add(0, 1, -1, 0)
+    send(6, 1, -1, 0, down)
+    add(1, 1, 1, 1)
+    send(7, 1, 1, 1, up)
+    pair(0, 1)
+    pair(0, -1)
+    add(2, 0, 1, 0)
+    send(10, 0, 1, 0, up)
+    add(3, 0, -1, 1)
+    send(11, 0, -1, 1, down)
+    pair(1, 0)
+    add(6, 1, 0, 0)
+    send(12, 1, 0, 0, across)
+    add(7, 1, 0, 1)
+    send(13, 1, 0, 1, across)
+    add(4, 0, -1, 0)
+    send(8, 0, -1, 0, down)
+    add(5, 0, 1, 1)
+    send(9, 0, 1, 1, up)
+    pair(0, 0)
+    for half, parts in ((0, (10, 8, 12)), (1, (11, 9, 13))):
+        total = piece(0, 0, half)[...].astype(f32)
+        for k in parts:
+            links.arrived(k, arrivals.at[k])
+            total += arrivals[k].astype(f32)
+        for t in range(2):
+            rows = pl.ds((2 * half + t) * EDGE, EDGE)
+            out[rows] = (self_term[rows] + jnp.transpose(total[t])).astype(bf16)
+    links.drain()
+
+
+def remote_call(kernel, collective_id, out_shape, in_spaces, out_spaces, scratch, copies, extra=()):
+    spec = lambda space: pl.BlockSpec(memory_space=space)
+    return pl.pallas_call(
+        kernel,
+        out_shape=out_shape,
+        in_specs=[spec(space) for space in in_spaces],
+        out_specs=jax.tree.map(spec, out_spaces),
+        scratch_shapes=[
+            *scratch,
+            pltpu.SemaphoreType.DMA((copies,)),
+            pltpu.SemaphoreType.DMA((copies,)),
+            *extra,
+        ],
+        compiler_params=pltpu.CompilerParams(
+            collective_id=collective_id, has_side_effects=True, vmem_limit_bytes=48 << 20
+        ),
+    )
+
+
 def local(features, adj_tiles, tile_rows, tile_cols, tile_count, w_neigh, w_self, bias, out_grad):
     tiles = adj_tiles[0, 0]
     row_index = tile_rows[0, 0]
@@ -144,59 +510,71 @@
     n_blk, n_rep = lax.axis_size("blk"), lax.axis_size("rep")
     row_tiles = span * n_blk // EDGE
     col_tiles = span * n_rep // EDGE
-    per_span = span // EDGE
     f32, bf16 = jnp.float32, jnp.bfloat16
-
-    sources = lax.all_gather(features, "rep", axis=0, tiled=True).reshape(col_tiles, EDGE, width)
+    shaped = jax.ShapeDtypeStruct
+    VMEM, ANY = pltpu.VMEM, pl.ANY
+
     forward_plan = schedule(row_index, col_index, live_tiles, row_tiles)
     backward_plan = schedule(col_index, row_index, live_tiles, col_tiles)
-    partial, degree_part = tile_call(
+    sources = remote_call(
+        gather_kernel, 1, shaped((n_rep, 2, span // 2, width), bf16), [ANY], ANY, [], 30,
+        extra=[pltpu.SemaphoreType.DMA],
+    )(features.reshape(2, span // 2, width)).reshape(col_tiles, EDGE, width)
+    partial, degree = tile_call(
         forward_kernel,
         forward_plan,
         tiles,
         sources,
-        (
-            jax.ShapeDtypeStruct((row_tiles, EDGE, width), bf16),
-            jax.ShapeDtypeStruct((row_tiles, 16, EDGE), f32),
-        ),
+        (shaped((row_tiles, EDGE, width), bf16), shaped((row_tiles, 16, EDGE), f32)),
         (row_tiles, EDGE, width),
     )
-    aggregate = lax.psum_scatter(
-        partial.reshape(row_tiles * EDGE, width), "blk", scatter_dimension=0, tiled=True
-    ).astype(f32)
-    degree = lax.psum_scatter(
-        degree_part[:, 0].reshape(row_tiles * EDGE), "blk", scatter_dimension=0, tiled=True
-    )
-    divisor = jnp.maximum(degree, 1.0)
-    mean_rows = (aggregate / divisor[:, None]).astype(bf16)
-    pre = jnp.dot(mean_rows, w_neigh, preferred_element_type=f32)
-    pre = pre + jnp.dot(features, w_self, preferred_element_type=f32) + bias
-    activations = jax.nn.silu(pre).astype(bf16)
-    sigma = jax.nn.sigmoid(pre)
-    d_pre = (out_grad.astype(f32) * sigma * (1.0 + pre * (1.0 - sigma))).astype(bf16)
-    neigh_local = lax.dot_general(mean_rows, d_pre, OVER_ROWS, preferred_element_type=f32)
-    self_local = lax.dot_general(features, d_pre, OVER_ROWS, preferred_element_type=f32)
-    bias_local = jnp.sum(d_pre.astype(f32), axis=0)
-    grad_w_neigh, grad_w_self, grad_bias = lax.psum(
-        (neigh_local, self_local, bias_local), ("blk", "rep")
-    )
-    mean_own = lax.dot_general(w_neigh, d_pre, OVER_COLS, preferred_element_type=f32)
-    mean_own = (mean_own / divisor[None, :]).astype(bf16)
-    mean_own = mean_own.reshape(width, per_span, EDGE).transpose(1, 0, 2)
-    grads = lax.all_gather(mean_own, "blk", axis=0, tiled=True)
-    back_part = tile_call(
+    two = (2, EDGE, width)
+    two_t = (2, width, EDGE)
+    act, grads, self_term, weight_grads, bias_grad = remote_call(
+        middle_kernel,
+        2,
+        (
+            shaped((span, width), bf16),
+            shaped((row_tiles, width, EDGE), bf16),
+            shaped((span, width), f32),
+            shaped((n_rep, 32, width), f32),
+            shaped((8, width), f32),
+        ),
+        [VMEM] * 7,
+        (VMEM, ANY, VMEM, VMEM, VMEM),
+        [
+            VMEM((2, 6, *two), bf16),
+            VMEM((2, 2, *two), bf16),
+            VMEM((2, *two), bf16),
+            VMEM((2, *two), bf16),
+            VMEM((2, *two), bf16),
+            VMEM((n_blk, 4, 16, EDGE), f32),
+            VMEM((span, width), bf16),
+            VMEM((span, width), bf16),
+            VMEM((4, width, EDGE), bf16),
+            VMEM((2, *two_t), bf16),
+            VMEM((n_rep, 48, width), bf16),
+            VMEM((n_rep, 48, width), bf16),
+            VMEM((48, width), bf16),
+            VMEM((n_blk, 48, width), bf16),
+        ],
+        D_ALL,
+        extra=[pltpu.SemaphoreType.DMA((2,))],
+    )(partial, degree, features, out_grad, w_neigh, w_self, bias.reshape(1, width))
+    back = tile_call(
         backward_kernel,
         backward_plan,
         tiles,
         grads,
-        jax.ShapeDtypeStruct((col_tiles, width, EDGE), bf16),
+        shaped((col_tiles, width, EDGE), bf16),
         (col_tiles, width, EDGE),
     )
-    back = lax.psum_scatter(back_part, "rep", scatter_dimension=0, tiled=True)
-    back = back.transpose(0, 2, 1).reshape(span, width).astype(f32)
-    grad_features = lax.dot_general(d_pre, w_self, OVER_COLS, preferred_element_type=f32)
-    grad_features = (grad_features + back).astype(bf16)
-    return (activations, grad_features, grad_w_neigh, grad_w_self, grad_bias)
+    grad_features = remote_call(
+        scatter_kernel, 3, shaped((span, width), bf16), [VMEM, VMEM], VMEM,
+        [VMEM((8, 4, width, EDGE), bf16), VMEM((14, *two_t), bf16)], 22,
+    )(back, self_term)
+    weight_grads = weight_grads.reshape(2, width, width)
+    return act, grad_features, weight_grads[0], weight_grads[1], bias_grad[0]
 
 
 def solution(mesh):

time: 427 us -> 165 us (0.39)
  waiting for transfers between devices: 245 us -> 0 us
  blocking collectives: 117 us -> 0 us
  Pallas kernels: 25.1 us -> 140 us
  between operations: 15.2 us -> 1.43 us
  matrix products: 5.65 us -> 0 us
  local copies, waits for them, and re-layouts: 7.74 us -> 12.3 us
    pallas_call x0 -> x3, Pallas kernels: none -> 105 us  [the longest x1 58.7 us: local(): remote_call(middle_kernel, 2, (shaped((span, width), bf16), shaped((row_t...]
    reduce_scatter x2 -> x0, waiting for transfers between devices: 99.9 us -> none  [the longest x1 66.1 us: local(): back = lax.psum_scatter(back_part, 'rep', scatter_dimension=0, tiled=True)]
    all_gather x2 -> x0, waiting for transfers between devices: 81.2 us -> none  [the longest x1 49.1 us: local(): grads = lax.all_gather(mean_own, 'blk', axis=0, tiled=True)]
    psum x1 -> x0, blocking collectives: 72.8 us -> none  [local(): lax.psum((neigh_local, self_local, bias_local), ('blk', 'rep'))]
    psum x1 -> x0, waiting for transfers between devices: 62.7 us -> none  [local(): lax.psum((neigh_local, self_local, bias_local), ('blk', 'rep'))]
    unnamed x1 -> x0, blocking collectives: 43.9 us -> none
    pallas_call x2, Pallas kernels: 25.1 us -> 34.9 us  [tile_call(): pl.pallas_call(kernel, out_shape=out_shape, in_specs=[smem] * 4 + [hbm, h...]
    dot_general x6 -> x0, matrix products: 5.65 us -> none  [the longest x1 1.22 us: local(): pre = jnp.dot(mean_rows, w_neigh, preferred_element_type=f32)]
  transfers between devices with their start and end apart: 5 -> 0, of which waited for: 5 -> 0; matrix products, arithmetic and copies ran while one was open for 4% -> 0% of each run, Pallas kernels for 3% -> 0%
where the time goes in v2:
time: 165 us; the launch traced here: 163 us
  Pallas kernels  140 us (85%)
  local copies, waits for them, and re-layouts  12.3 us (7%)
  other arithmetic  8.85 us (5%)
    pallas_call x1, Pallas kernels, local(): remote_call(middle_kernel, 2, (shaped((span, width), bf16), shaped((row_t...  58.7 us
    pallas_call x2, Pallas kernels, tile_call(): pl.pallas_call(kernel, out_shape=out_shape, in_specs=[smem] * 4 + [hbm, h...  34.9 us
    pallas_call x1, Pallas kernels, local(): remote_call(scatter_kernel, 3, shaped((span, width), bf16), [VMEM, VMEM],...  23.6 us
    pallas_call x1, Pallas kernels, local(): remote_call(gather_kernel, 1, shaped((n_rep, 2, span // 2, width), bf16),...  23.1 us
    unnamed x22, local copies, waits for them, and re-layouts  8.74 us

profile of v2, /device:TPU:2, one launch (start us, length us, event | category | flops | bytes accessed | tf_op | source)
XLA Modules:
  0.0 162.9 jit_solution(17890414260848887592)
XLA Ops:
  1.3 0.8 convert_reduce_fusion.2
  2.1 0.8 convert_reduce_fusion.3
  2.9 0.6 fusion.11
  3.5 0.7 fusion.10
  4.2 0.8 select_reduce_fusion.2
  5.0 0.8 select_reduce_fusion.3
  5.8 1.0 convert_reduce_fusion.1
  6.8 1.0 convert_reduce_fusion
  7.8 0.7 add_add_fusion
  9.5 0.8 slice.17.key_ref
  10.9 0.8 slice.18.key_ref
  11.7 0.9 copy-done.3
  12.7 23.1 %shard_map.128 = bf16[16,2,256,256]{3,2,1,0:T(8,128)(2,1)S(1)} custom-call(bf16[2,256,256]{2,1,0:T(8,128)(2,1)S(1)} %bitcast.15), custom_call_target="tpu_custom_call" | custom-call | tf_op jit(solution)/shard_map/pallas_call | solution.py:519
  35.8 1.9 %copy-done.1 = bf16[16,2,256,256]{3,2,1,0:T(8,128)(2,1)} copy-done((bf16[16,2,256,256]{3,2,1,0:T(8,128)(2,1)}, bf16[16,2,256,256]{3,2,1,0:T(8,128)(2,1)S(1)}, u32[]{:S(2)}) %copy-start.1) | copy-done | bytes 4194328
  38.4 15.7 %shard_map.129 = (bf16[32,128,256]{2,1,0:T(8,128)(2,1)}, f32[32,16,128]{2,1,0:T(8,128)}) custom-call(s32[608]{0:T(1024)} %get-tuple-element.32.slot_ref, s32[608]{0:T(1024)} %get-tuple-element.31.other_ref, s32[152]{0:T(256)} %slice.17.key_ref, s32[1]{0:T(128)} %bitcast.3.total_ref, bf16[512,128,128]{2,1,0:T(8,128)(2,1)} %bitcast.17, ...), custom_call_target="tpu_custom_call" | custom-call | tf_op jit(solution)/shard_map/pallas_call | solution.py:125
  54.2 0.9 copy-done.6
  55.1 58.7 %shard_map.130 = (bf16[512,256]{1,0:T(8,128)(2,1)S(1)}, bf16[32,256,128]{2,1,0:T(8,128)(2,1)S(1)}, f32[512,256]{1,0:T(8,128)S(1)}, f32[16,32,256]{2,1,0:T(8,128)S(1)}, f32[8,256]{1,0:T(8,128)S(1)}) custom-call(bf16[32,128,256]{2,1,0:T(8,128)(2,1)} %get-tuple-element.12.partial, f32[32,16,128]{2,1,0:T(8,128)S(1)} %copy-done.6, ...), custom_call_target="tpu_custom_call" | custom-call | tf_op jit(solution)/shard_map/pallas_call | solution.py:533
  113.8 1.3 copy-done.2
  115.7 0.8 fusion.12
  116.6 19.1 %shard_map.131.back = bf16[64,256,128]{2,1,0:T(8,128)(2,1)} custom-call(s32[704]{0:T(1024)} %get-tuple-element.27.slot_ref, s32[704]{0:T(1024)} %get-tuple-element.26.other_ref, s32[176]{0:T(256)} %slice.18.key_ref, s32[1]{0:T(128)} %bitcast.8.total_ref, bf16[512,128,128]{2,1,0:T(8,128)(2,1)} %bitcast.18, bf16[128,128]{1,0:T(8,128)(2,1)} %broadcast_10_zero_tile.2.zero_tile, ...), custom_call_target="tpu_custom_call" | custom-call | tf_op jit(solution)/shard_map/pallas_call | solution.py:125
  135.7 2.2 %copy-done = bf16[64,256,128]{2,1,0:T(8,128)(2,1)S(1)} copy-done((bf16[64,256,128]{2,1,0:T(8,128)(2,1)S(1)}, bf16[64,256,128]{2,1,0:T(8,128)(2,1)}, u32[]{:S(2)}) %copy-start) | copy-done | bytes 4194328
  137.9 23.6 %shard_map.132 = bf16[512,256]{1,0:T(8,128)(2,1)S(1)} custom-call(bf16[64,256,128]{2,1,0:T(8,128)(2,1)S(1)} %copy-done, f32[512,256]{1,0:T(8,128)S(1)} %get-tuple-element.16.self_term), custom_call_target="tpu_custom_call" | custom-call | tf_op jit(solution)/shard_map/pallas_call | solution.py:572
  161.5 0.7 copy.17
  162.2 0.7 copy.18
  (23 shorter events, 2.9 us)
Async XLA Ops:
  11.7 0.9 copy-start.3
  35.8 1.9 %copy-start.1 = (bf16[16,2,256,256]{3,2,1,0:T(8,128)(2,1)}, bf16[16,2,256,256]{3,2,1,0:T(8,128)(2,1)S(1)}, u32[]{:S(2)}) copy-start(bf16[16,2,256,256]{3,2,1,0:T(8,128)(2,1)S(1)} %shard_map.128) | copy-start | bytes 12582916
  38.3 15.8 %copy-start.4 = (bf16[512,256]{1,0:T(8,128)(2,1)S(1)}, bf16[512,256]{1,0:T(8,128)(2,1)}, u32[]{:S(2)}) copy-start(bf16[512,256]{1,0:T(8,128)(2,1)} %features.1) | copy-start | bytes 786436
  38.3 15.8 %copy-start.5 = (bf16[512,256]{1,0:T(8,128)(2,1)S(1)}, bf16[512,256]{1,0:T(8,128)(2,1)}, u32[]{:S(2)}) copy-start(bf16[512,256]{1,0:T(8,128)(2,1)} %out_grad.1) | copy-start | bytes 786436
  38.3 15.8 %copy-start.7 = (bf16[256,256]{1,0:T(8,128)(2,1)S(1)}, bf16[256,256]{1,0:T(8,128)(2,1)}, u32[]{:S(2)}) copy-start(bf16[256,256]{1,0:T(8,128)(2,1)} %w_neigh.1) | copy-start | bytes 393220
  38.3 15.8 %copy-start.8 = (bf16[256,256]{1,0:T(8,128)(2,1)S(1)}, bf16[256,256]{1,0:T(8,128)(2,1)}, u32[]{:S(2)}) copy-start(bf16[256,256]{1,0:T(8,128)(2,1)} %w_self.1) | copy-start | bytes 393220
  38.3 15.8 %copy-start.9 = (f32[256]{0:T(256)S(1)}, f32[256]{0:T(256)}, u32[]{:S(2)}) copy-start(f32[256]{0:T(256)} %param.16) | copy-start | bytes 3076
  54.2 1.0 copy-start.6
  113.8 1.3 copy-start.2
  135.7 2.2 %copy-start = (bf16[64,256,128]{2,1,0:T(8,128)(2,1)S(1)}, bf16[64,256,128]{2,1,0:T(8,128)(2,1)}, u32[]{:S(2)}) copy-start(bf16[64,256,128]{2,1,0:T(8,128)(2,1)} %shard_map.131.back) | copy-start | bytes 12582916

commit v3 on v0

v3 whole, which is shorter than its diff:
```python
import functools

import jax
import jax.numpy as jnp
from jax import lax
from jax.experimental import pallas as pl
from jax.experimental.pallas import tpu as pltpu
from jax.sharding import PartitionSpec as P

MESH = pl.DeviceIdType.MESH
EDGE = 128
GROUP = 4
UNROLL = 8
HALVES = 2
SLOTS = 512
ROW_TILES = 32
COL_TILES = 64
N_BLK = 8
N_REP = 16
OVER_ROWS = (((0,), (0,)), ((), ()))
OVER_COLS = (((1,), (1,)), ((), ()))
f32, bf16, i32 = jnp.float32, jnp.bfloat16, jnp.int32


def body_count(groups):
    steps = SLOTS // GROUP + groups * (GROUP - 1) // GROUP
    return -(-steps // UNROLL)


F_BODIES, B_BODIES = body_count(ROW_TILES), body_count(COL_TILES)
STEPS = max(F_BODIES, B_BODIES) * UNROLL
PLACES = -(-STEPS * GROUP // EDGE) * EDGE

S_DEGREE = 0
S_GATHER, S_SUM, S_GRADS, S_BACK, S_HALF = 0, 30, 43, 56, 78
S_FIRST = 8
S_REP = S_FIRST + HALVES * S_HALF
S_BLK = S_REP + N_REP
S_OUT = S_BLK + N_BLK
S_ALL = S_OUT + N_REP


def write_plan(keys, others, live, plan, row, bodies):
    iota = lambda shape, axis: lax.broadcasted_iota(i32, shape, axis)
    square = (EDGE, EDGE)
    tall = (SLOTS, EDGE)

    def stand(v):
        return jnp.transpose(jnp.broadcast_to(v, (EDGE, v.shape[1])))

    def count_of(hits, axis):
        return jnp.sum(jnp.where(hits, 1, 0), axis=axis, keepdims=True)

    key, other = stand(keys), stand(others)
    slot, lane = iota(tall, 0), iota(tall, 1)
    alive = slot < live
    wide = (SLOTS, SLOTS)
    before = (jnp.concatenate([key] * (SLOTS // EDGE), axis=1) == keys) & (iota(wide, 1) < iota(wide, 0))
    rank = count_of(before, 1)
    counts = count_of((key == lane) & alive, 0)
    steps = (counts + (GROUP - 1)) // GROUP
    steps_down = stand(steps)
    base = jnp.sum(jnp.where(iota(square, 0) < iota(square, 1), steps_down, 0), axis=0, keepdims=True)
    base_down = stand(base)
    base_of = jnp.sum(jnp.where(key == lane, base, 0), axis=1, keepdims=True)
    place = jnp.where(alive, base_of * GROUP + rank, -1)
    code = slot * COL_TILES + other + 1
    for c in range(-(-bodies * UNROLL * GROUP // EDGE)):
        here = pl.ds(c * EDGE, EDGE)
        found = jnp.sum(jnp.where(place == lane + c * EDGE, code, 0), axis=0, keepdims=True)
        plan[row : row + 1, here] = jnp.where(found > 0, (found - 1) // COL_TILES, SLOTS)
        plan[row + 1 : row + 2, here] = jnp.where(found > 0, (found - 1) % COL_TILES, 0)
    for c in range(-(-bodies * UNROLL // EDGE)):
        first = count_of((base_down == iota(square, 1) + c * EDGE) & (steps_down > 0), 0)
        plan[row + 2 : row + 3, pl.ds(c * EDGE, EDGE)] = 1 - first
    plan[row + 3 : row + 4, pl.ds(0, EDGE)] = jnp.where(steps > 0, base + steps - 1, -1)


class Links:
    def __init__(self, send_sems, recv_sems):
        self.send_sems, self.recv_sems, self.sent = send_sems, recv_sems, []

    def send(self, k, source, target, device, like):
        pltpu.make_async_remote_copy(
            src_ref=source,
            dst_ref=target,
            send_sem=self.send_sems.at[k],
            recv_sem=self.recv_sems.at[k],
            device_id=device,
            device_id_type=MESH,
        ).start()
        self.sent.append((k, like))

    def arrived(self, k, target):
        pltpu.make_async_copy(target, target, self.recv_sems.at[k]).wait()

    def drain(self):
        for k, like in self.sent:
            pltpu.make_async_copy(like, like, self.send_sems.at[k]).wait()


def layer_kernel(
    features, feature_tiles, tiles, rows_in, cols_in, count_in, w_neigh_in, w_self_in, bias_in, out_grad_in,
    act, grad_features, weight_grads, bias_grad,
    buf, sources_0, sources_1, grads_0, grads_1, steps_out, total, degree_total, degree_steps,
    partial, degree, degrees, from_y, sums, to_x, from_x, own_grads, back, paired, arrivals,
    feats, out_grad, w_neigh, w_self, bias, mean, d_pre, self_term,
    rep_out, rep_in, blk_out, blk_in, ints, plan, count, plan_s,
    send_sems, recv_sems, load_sems, plan_sem,
):
    blk, rep = lax.axis_index("blk"), lax.axis_index("rep")
    y, x, z, core = blk // 2, (blk % 2) * 2 + rep // 8, (rep // 2) % 4, rep % 2
    x_hi, x_lo = blk % 2, rep // 8
    sources, grads = (sources_0, sources_1), (grads_0, grads_1)
    links = Links(send_sems, recv_sems)
    piece_like = sources_0.at[pl.ds(0, 2)]
    chunk_like = sources_0.at[pl.ds(0, 4)]

    def device(dy=0, dx=0, dz=0, sibling=False, partner=False):
        to_y, to_z = (y + dy) % 4, (z + dz) % 4
        to_x = x + 1 - 2 * (x % 2) if partner else (x + dx) % 4
        to_core = 1 - core if sibling else core
        return (to_y * 2 + to_x // 2, (to_x % 2) * 8 + to_z * 2 + to_core)

    y_up, y_down, z_up, z_down = device(dy=1), device(dy=-1), device(dz=1), device(dz=-1)
    across, sibling, far_x = device(partner=True), device(sibling=True), device(dx=2)
    blk_peer = lambda d: ((blk + d) % N_BLK, rep)
    rep_peer = lambda d: (blk, (rep + d) % N_REP)

    loads = []

    def load(source, target):
        copy = pltpu.make_async_copy(source, target, load_sems.at[len(loads)])
        copy.start()
        loads.append(copy)
        return copy

    own_block = pl.ds(rep * 4, 4)
    own_loads = [load(feature_tiles.at[:, :, pl.ds(h * EDGE, EDGE)], sources[h].at[own_block]) for h in range(HALVES)]
    int_loads = [load(rows_in, ints.at[pl.ds(0, 1)]), load(cols_in, ints.at[pl.ds(1, 1)]), load(count_in, count)]
    some = SLOTS // 8
    tile_loads = [load(tiles.at[pl.ds(n * some, some)], buf.at[pl.ds(n * some, some)]) for n in range(8)]
    node_loads = [
        load(features, feats), load(out_grad_in, out_grad), load(w_neigh_in, w_neigh),
        load(w_self_in, w_self), load(bias_in, bias),
    ]

    barrier = pltpu.get_barrier_semaphore()
    peers = [far_x] + [blk_peer(d) for d in range(1, N_BLK)] + [rep_peer(d) for d in range(1, N_REP)]
    for peer in peers:
        pl.semaphore_signal(barrier, inc=1, device_id=peer, device_id_type=MESH)
    pl.semaphore_wait(barrier, len(peers))

    def rep_block(dx, dz, half, other_core=False):
        index = ((x_lo + dx) % 2) * 8 + ((z + dz) % 4) * 2 + (1 - core if other_core else core)
        return pl.ds(index * 4 + 2 * half, 2)

    def sem(h, run, k):
        return S_FIRST + h * S_HALF + run + k

    gather_own = {0: (0, z_up), 1: (1, z_down), 2: (0, across), 3: (1, across), 4: (1, z_up), 5: (0, z_down)}
    gather_steps = {
        0: (-1, 0, 0, (6, z_up)),
        1: (1, 0, 1, (7, z_down)),
        2: (0, 1, 0, (8, z_up)),
        3: (0, 1, 1, (9, z_down)),
        4: (-1, 0, 1, (10, across)),
        5: (1, 0, 0, (11, across)),
        6: (2, 0, 0, None),
        7: (2, 0, 1, None),
        8: (-1, 1, 0, (12, z_up)),
        9: (1, 1, 1, (13, z_down)),
        10: (-1, 1, 1, None),
        11: (1, 1, 0, None),
        12: (2, 1, 0, None),
        13: (2, 1, 1, None),
    }

    def gather_start(h, *ks):
        for k in ks:
            half, where = gather_own[k]
            piece = sources[h].at[rep_block(0, 0, half)]
            links.send(sem(h, S_GATHER, k), piece, piece, where, piece_like)

    def gather_sibling(h):
        for half in range(2):
            piece = sources[h].at[rep_block(0, 0, half)]
            links.send(sem(h, S_GATHER, 14 + half), piece, piece, sibling, piece_like)

    def gather(h, *ks):
        for k in ks:
            dz, dx, half, onward = gather_steps[k]
            piece = sources[h].at[rep_block(dx, dz, half)]
            links.arrived(sem(h, S_GATHER, k), piece)
            if onward is not None:
                links.send(sem(h, S_GATHER, onward[0]), piece, piece, onward[1], piece_like)
            links.send(sem(h, S_GATHER, 16 + k), piece, piece, sibling, piece_like)

    def gather_end(h):
        for half in range(2):
            links.arrived(sem(h, S_GATHER, 14 + half), sources[h].at[rep_block(0, 0, half, True)])
        for k, (dz, dx, half, _) in gather_steps.items():
            links.arrived(sem(h, S_GATHER, 16 + k), sources[h].at[rep_block(dx, dz, half, True)])

    for copy in own_loads:
        copy.wait()
    gather_start(0, 0, 1, 2, 3, 4, 5)
    gather_sibling(0)
    gather_start(1, 0, 1, 2, 3)

    for copy in int_loads:
        copy.wait()
    live = count[0, 0]
    row_keys, col_keys = ints[0:1], ints[1:2]
    write_plan(row_keys, col_keys, live, plan, 0, F_BODIES)
    gather(0, 2, 3, 0, 1)
    gather_start(1, 4, 5)
    gather_sibling(1)
    write_plan(col_keys, row_keys, live, plan, 4, B_BODIES)
    plan_copy = pltpu.make_async_copy(plan, plan_s, plan_sem)
    plan_copy.start()
    buf[SLOTS] = jnp.zeros((EDGE, EDGE), bf16)
    gather(0, 4, 5)
    gather(1, 2, 3)
    gather(0, 8, 9)
    gather(1, 0, 1)
    gather(0, 6, 7, 10, 11)
    gather(1, 4, 5)
    gather(0, 12, 13)
    for copy in tile_loads:
        copy.wait()
    plan_copy.wait()
    gather_end(0)

    def tile_pass(row, bodies, product, extra=None, hooks=()):
        total[...] = jnp.zeros_like(total)

        @pl.loop(0, bodies)
        def _(body):
            value = total[...]
            for k in range(UNROLL):
                n = body * UNROLL + k
                places = [n * GROUP + m for m in range(GROUP)]
                held = [buf[plan_s[row, p]] for p in places]
                keep = plan_s[row + 2, n].astype(f32)
                value = value * keep + product(held, [plan_s[row + 1, p] for p in places])
                steps_out[n] = value.astype(bf16)
                if extra is not None:
                    extra(n, keep, held)
            total[...] = value
            for when, action in hooks:
                pl.when(body == when)(action)

    def collect(row, count, target):
        @pl.loop(0, count)
        def _(n):
            at = plan_s[row + 3, n]
            has = jnp.where(at >= 0, 1.0, 0.0)
            target[n] = (steps_out[jnp.maximum(at, 0)].astype(f32) * has).astype(bf16)

    ones = jnp.ones((16, EDGE), bf16)

    def forward(h):
        def product(held, others):
            left = jnp.concatenate(held, axis=1)
            right = jnp.concatenate([sources[h][o] for o in others], axis=0)
            return jnp.dot(left, right, preferred_element_type=f32)

        return product

    def row_sums(n, keep, held):
        marks = (held[0] + held[1]) + (held[2] + held[3])
        sums_here = lax.dot_general(ones, marks, OVER_COLS, preferred_element_type=f32)[0:8]
        degree_total[...] = degree_total[...] * keep + sums_here
        degree_steps[n] = degree_total[...]

    degree_total[...] = jnp.zeros_like(degree_total)
    tile_pass(
        0, F_BODIES, forward(0), row_sums,
        hooks=(
            (4, lambda: gather(1, 8, 9)),
            (9, lambda: gather(1, 6, 7, 10, 11)),
            (14, lambda: gather(1, 12, 13)),
        ),
    )
    collect(0, ROW_TILES, partial.at[0])

    @pl.loop(0, ROW_TILES)
    def _(n):
        at = plan_s[3, n]
        degree[n] = degree_steps[jnp.maximum(at, 0)] * jnp.where(at >= 0, 1.0, 0.0)

    def blk_block(dy, j):
        return ((y + dy) % 4) * 2 + (x_hi if j else 1 - x_hi)

    def part(h, dy, j, half):
        return partial.at[h, pl.ds(blk_block(dy, j) * 4 + 2 * half, 2)]

    def wide(ref):
        return ref[...].astype(f32)

    def sum_far(h, j):
        links.send(sem(h, S_SUM, 6 * j), part(h, 2, j, 0), from_y.at[h, j, 0], y_up, piece_like)
        links.send(sem(h, S_SUM, 6 * j + 1), part(h, 2, j, 1), from_y.at[h, j, 1], y_down, piece_like)

    def sum_near(h, j):
        links.send(sem(h, S_SUM, 6 * j + 2), part(h, 1, j, 1), from_y.at[h, j, 2], y_up, piece_like)
        links.send(sem(h, S_SUM, 6 * j + 3), part(h, -1, j, 0), from_y.at[h, j, 3], y_down, piece_like)

    def sum_combine(h, j):
        for half, dy, where in ((0, 1, y_up), (1, -1, y_down)):
            links.arrived(sem(h, S_SUM, 6 * j + half), from_y.at[h, j, half])
            sums[h, j, half] = (wide(from_y.at[h, j, half]) + wide(part(h, dy, j, half))).astype(bf16)
            links.send(
                sem(h, S_SUM, 6 * j + 4 + half), sums.at[h, j, half], from_y.at[h, j, 4 + half], where, piece_like
            )

    def sum_y(h, j, half):
        near, far = (3, 4) if half == 0 else (2, 5)
        for slot in (near, far):
            links.arrived(sem(h, S_SUM, 6 * j + slot), from_y.at[h, j, slot])
        return wide(part(h, 0, j, half)) + wide(from_y.at[h, j, near]) + wide(from_y.at[h, j, far])

    def sum_across(h):
        for half in range(2):
            to_x[h, 2 * half : 2 * half + 2] = sum_y(h, 0, half).astype(bf16)
        links.send(sem(h, S_SUM, 12), to_x.at[h], from_x.at[h], far_x, chunk_like)

    sum_far(0, 0)
    sum_far(0, 1)
    sum_near(0, 0)
    for d in range(1, N_BLK):
        to = (blk + d) % N_BLK
        links.send(S_DEGREE + d, degree.at[pl.ds(to * 4, 4)], degrees.at[d], blk_peer(d), degrees.at[0])
    gather_end(1)

    def sum_middle(h):
        sum_combine(h, 0)
        sum_near(h, 1)

    tile_pass(
        0, F_BODIES, forward(1),
        hooks=((10, lambda: sum_middle(0)), (14, lambda: sum_combine(0, 1))),
    )
    collect(0, ROW_TILES, partial.at[1])
    sum_far(1, 0)
    sum_far(1, 1)
    sum_near(1, 0)
    sum_across(0)
    sum_middle(1)
    sum_combine(1, 1)
    for copy in node_loads:
        copy.wait()
    for d in range(1, N_BLK):
        links.arrived(S_DEGREE + d, degrees.at[d])
    degree_sum = degree[pl.ds(blk * 4, 4)]
    for d in range(1, N_BLK):
        degree_sum += degrees[d]
    divisor = jnp.maximum(degree_sum, 1.0)
    from_self = jnp.dot(feats[...], w_self[...], preferred_element_type=f32) + bias[...]
    self_term[...] = from_self
    sum_across(1)

    def grads_at(h, dy, j, half):
        return grads[h].at[pl.ds(blk_block(dy, j) * 4 + 2 * half, 2)]

    for half in range(2):
        whole = []
        for h in range(HALVES):
            value = sum_y(h, 1, half)
            if half == 0:
                links.arrived(sem(h, S_SUM, 12), from_x.at[h])
            whole.append(value + from_x[h, 2 * half : 2 * half + 2].astype(f32))
        for t in (2 * half, 2 * half + 1):
            here = pl.ds(t * EDGE, EDGE)
            lanes = divisor[t, 0:1]
            down = jnp.transpose(jnp.broadcast_to(lanes, (EDGE, EDGE)))
            mean_rows = jnp.concatenate([w[t - 2 * half] / down for w in whole], axis=1).astype(bf16)
            pre = jnp.dot(mean_rows, w_neigh[...], preferred_element_type=f32) + self_term[here]
            sigma = jax.nn.sigmoid(pre)
            act[here] = (pre * sigma).astype(bf16)
            d_here = (out_grad[here].astype(f32) * sigma * (1.0 + pre * (1.0 - sigma))).astype(bf16)
            mean[here] = mean_rows
            d_pre[here] = d_here
            down_grad = lax.dot_general(w_neigh[...], d_here, OVER_COLS, preferred_element_type=f32)
            down_grad = (down_grad / lanes).astype(bf16)
            for h in range(HALVES):
                own_grads[h, t] = down_grad[h * EDGE : (h + 1) * EDGE]

    def grads_own(h):
        block = pl.ds(blk * 4, 4)
        grads[h][block] = own_grads[h]
        links.send(sem(h, S_GRADS, 12), own_grads.at[h], grads[h].at[block], far_x, chunk_like)

    def grads_along(h, j):
        base = 6 * (1 - j)
        for k, half, where in ((0, 0, y_up), (1, 1, y_down), (3, 1, y_up), (2, 0, y_down)):
            piece = grads_at(h, 0, j, half)
            links.send(sem(h, S_GRADS, base + k), piece, piece, where, piece_like)

    def grads_onward(h, j):
        base = 6 * (1 - j)
        for k, dy, half, where in ((0, -1, 0, y_up), (1, 1, 1, y_down)):
            piece = grads_at(h, dy, j, half)
            links.arrived(sem(h, S_GRADS, base + k), piece)
            links.send(sem(h, S_GRADS, base + 4 + k), piece, piece, where, piece_like)

    def grads_other(h):
        links.arrived(sem(h, S_GRADS, 12), grads[h].at[pl.ds(blk_block(0, 0) * 4, 4)])
        grads_along(h, 0)

    def grads_end(h):
        for j in range(2):
            base = 6 * (1 - j)
            for k, dy, half in ((2, 1, 0), (3, -1, 1), (4, 2, 0), (5, 2, 1)):
                links.arrived(sem(h, S_GRADS, base + k), grads_at(h, dy, j, half))

    grads_own(0)
    grads_along(0, 1)
    grads_own(1)

    which = lax.broadcasted_iota(i32, (16, 2 * EDGE), 0)

    def two_rows(v):
        high = v.astype(bf16).astype(f32)
        return jnp.where(which == 0, high, jnp.where(which == 1, v - high, 0.0)).astype(bf16)

    neigh = lax.dot_general(mean[...], d_pre[...], OVER_ROWS, preferred_element_type=f32)
    for p in range(8):
        rep_out[p, 0:32] = neigh[32 * p : 32 * p + 32].astype(bf16)
    grads_onward(0, 1)
    grads_along(1, 1)
    own = lax.dot_general(feats[...], d_pre[...], OVER_ROWS, preferred_element_type=f32)
    for p in range(8):
        rep_out[8 + p, 0:32] = own[32 * p : 32 * p + 32].astype(bf16)
    own_bias = two_rows(jnp.sum(d_pre[...].astype(f32), axis=0, keepdims=True))
    for p in range(N_REP):
        rep_out[p, 32:48] = own_bias
    for d in range(1, N_REP):
        links.send(S_REP + d, rep_out.at[(rep + d) % N_REP], rep_in.at[d], rep_peer(d), rep_in.at[0])
    rep_in[0] = rep_out[rep]
    grads_other(0)
    grads_onward(1, 1)
    self_term[...] = lax.dot_general(d_pre[...], w_self[...], OVER_COLS, preferred_element_type=f32)

    for d in range(1, N_REP):
        links.arrived(S_REP + d, rep_in.at[d])
    summed = rep_in[rep].astype(f32)
    for source in range(1, N_REP):
        summed += rep_in[(rep + N_REP - source) % N_REP].astype(f32)
    blk_out[0:32] = summed[0:32].astype(bf16)
    blk_out[32:48] = two_rows(summed[32:33] + summed[33:34])
    for d in range(1, N_BLK):
        links.send(S_BLK + d, blk_out, blk_in.at[d], blk_peer(d), blk_in.at[0])
    blk_in[0] = blk_out[...]
    grads_onward(0, 0)
    grads_other(1)

    def weights_end():
        for d in range(1, N_BLK):
            links.arrived(S_BLK + d, blk_in.at[d])
        summed = blk_in[blk].astype(f32)
        for source in range(1, N_BLK):
            summed += blk_in[(blk + N_BLK - source) % N_BLK].astype(f32)
        weight_grads[rep] = summed[0:32]
        bias_grad[...] = jnp.broadcast_to(summed[32:33] + summed[33:34], bias_grad.shape)
        for d in range(1, N_REP):
            links.send(S_OUT + d, weight_grads.at[rep], weight_grads.at[rep], rep_peer(d), weight_grads.at[0])

    weights_end()
    grads_end(0)

    def backward(h):
        def product(held, others):
            left = jnp.concatenate([grads[h][o] for o in others], axis=1)
            right = jnp.concatenate(held, axis=0)
            return jnp.dot(left, right, preferred_element_type=f32)

        return product

    tile_pass(4, B_BODIES, backward(0), hooks=((2, lambda: grads_onward(1, 0)),))
    collect(4, COL_TILES, back.at[0])

    order = ((1, 2), (1, 1), (1, -1), (0, 2), (0, 1), (0, -1), (1, 0), (0, 0))

    def back_block(dx, dz, other_core):
        index = ((x_lo + dx) % 2) * 8 + ((z + dz) % 4) * 2 + (1 - core if other_core else core)
        return pl.ds(index * 4, 4)

    def back_start(h):
        for n, (dx, dz) in enumerate(order):
            links.send(
                sem(h, S_BACK, 14 + n), back.at[h, back_block(dx, dz, True)], paired.at[h, n], sibling, chunk_like
            )

    def back_pair(h, dx, dz):
        n = order.index((dx, dz))
        links.arrived(sem(h, S_BACK, 14 + n), paired.at[h, n])
        paired[h, n] = (paired[h, n].astype(f32) + back[h, back_block(dx, dz, False)].astype(f32)).astype(bf16)

    def back_piece(h, dx, dz, half):
        return paired.at[h, order.index((dx, dz)), pl.ds(2 * half, 2)]

    def back_send(h, k, dx, dz, half, where):
        links.send(sem(h, S_BACK, k), back_piece(h, dx, dz, half), arrivals.at[h, k], where, piece_like)

    def back_add(h, k, dx, dz, half):
        links.arrived(sem(h, S_BACK, k), arrivals.at[h, k])
        ref = back_piece(h, dx, dz, half)
        ref[...] = (ref[...].astype(f32) + arrivals[h, k].astype(f32)).astype(bf16)

    def back_raw(h):
        back_start(h)
        back_pair(h, 1, 2)
        back_send(h, 0, 1, 2, 0, z_down)
        back_send(h, 1, 1, 2, 1, z_up)
        back_pair(h, 1, 1)
        back_send(h, 2, 1, 1, 0, across)
        back_pair(h, 1, -1)
        back_send(h, 3, 1, -1, 1, across)
        back_pair(h, 0, 2)
        back_send(h, 4, 0, 2, 0, z_down)
        back_send(h, 5, 0, 2, 1, z_up)
        for dx, dz in order[4:]:
            back_pair(h, dx, dz)

    def back_first(h):
        back_add(h, 0, 1, -1, 0)
        back_send(h, 6, 1, -1, 0, z_down)
        back_add(h, 1, 1, 1, 1)
        back_send(h, 7, 1, 1, 1, z_up)
        back_add(h, 2, 0, 1, 0)
        back_send(h, 10, 0, 1, 0, z_up)
        back_add(h, 3, 0, -1, 1)
        back_send(h, 11, 0, -1, 1, z_down)

    def back_second(h):
        back_add(h, 4, 0, -1, 0)
        back_send(h, 8, 0, -1, 0, z_down)
        back_add(h, 5, 0, 1, 1)
        back_send(h, 9, 0, 1, 1, z_up)

    def back_third(h):
        back_add(h, 6, 1, 0, 0)
        back_send(h, 12, 1, 0, 0, across)
        back_add(h, 7, 1, 0, 1)
        back_send(h, 13, 1, 0, 1, across)

    def back_end(h):
        for half, parts in ((0, (10, 8, 12)), (1, (11, 9, 13))):
            value = back_piece(h, 0, 0, half)[...].astype(f32)
            for k in parts:
                links.arrived(sem(h, S_BACK, k), arrivals.at[h, k])
                value += arrivals[h, k].astype(f32)
            for t in range(2):
                here, lanes = pl.ds((2 * half + t) * EDGE, EDGE), pl.ds(h * EDGE, EDGE)
                grad_features[here, lanes] = (self_term[here, lanes] + jnp.transpose(value[t])).astype(bf16)

    back_raw(0)
    grads_end(1)
    tile_pass(
        4, B_BODIES, backward(1),
        hooks=(
            (8, lambda: back_first(0)),
            (12, lambda: back_second(0)),
            (18, lambda: back_third(0)),
        ),
    )
    collect(4, COL_TILES, back.at[1])
    back_raw(1)
    back_first(1)
    back_second(1)
    back_third(1)
    back_end(0)
    back_end(1)
    for d in range(1, N_REP):
        links.arrived(S_OUT + d, weight_grads.at[(rep + N_REP - d) % N_REP])
    links.drain()


def local(features, adj_tiles, tile_rows, tile_cols, tile_count, w_neigh, w_self, bias, out_grad):
    span, width = features.shape
    shaped = jax.ShapeDtypeStruct
    VMEM = pltpu.VMEM
    square = (EDGE, EDGE)
    any_spec, vmem_spec = pl.BlockSpec(memory_space=pl.ANY), pl.BlockSpec(memory_space=VMEM)
    act, grad_features, weight_grads, bias_grad = pl.pallas_call(
        layer_kernel,
        out_shape=(
            shaped((span, width), bf16),
            shaped((span, width), bf16),
            shaped((N_REP, 32, width), f32),
            shaped((8, width), f32),
        ),
        in_specs=[any_spec] * 10,
        out_specs=(vmem_spec,) * 4,
        scratch_shapes=[
            VMEM((SLOTS + 1, *square), bf16),
            VMEM((COL_TILES, *square), bf16),
            VMEM((COL_TILES, *square), bf16),
            VMEM((ROW_TILES, *square), bf16),
            VMEM((ROW_TILES, *square), bf16),
            VMEM((STEPS, *square), bf16),
            VMEM(square, f32),
            VMEM((8, EDGE), f32),
            VMEM((F_BODIES * UNROLL, 8, EDGE), f32),
            VMEM((HALVES, ROW_TILES, *square), bf16),
            VMEM((ROW_TILES, 8, EDGE), f32),
            VMEM((N_BLK, 4, 8, EDGE), f32),
            VMEM((HALVES, 2, 6, 2, *square), bf16),
            VMEM((HALVES, 2, 2, 2, *square), bf16),
            VMEM((HALVES, 4, *square), bf16),
            VMEM((HALVES, 4, *square), bf16),
            VMEM((HALVES, 4, *square), bf16),
            VMEM((HALVES, COL_TILES, *square), bf16),
            VMEM((HALVES, 8, 4, *square), bf16),
            VMEM((HALVES, 14, 2, *square), bf16),
            VMEM((span, width), bf16),
            VMEM((span, width), bf16),
            VMEM((width, width), bf16),
            VMEM((width, width), bf16),
            VMEM((1, width), f32),
            VMEM((span, width), bf16),
            VMEM((span, width), bf16),
            VMEM((span, width), f32),
            VMEM((N_REP, 48, width), bf16),
            VMEM((N_REP, 48, width), bf16),
            VMEM((48, width), bf16),
            VMEM((N_BLK, 48, width), bf16),
            VMEM((8, SLOTS), i32),
            VMEM((8, PLACES), i32),
            pltpu.SMEM((1, 1), i32),
            pltpu.SMEM((8, PLACES), i32),
            pltpu.SemaphoreType.DMA((S_ALL,)),
            pltpu.SemaphoreType.DMA((S_ALL,)),
            pltpu.SemaphoreType.DMA((18,)),
            pltpu.SemaphoreType.DMA,
        ],
        compiler_params=pltpu.CompilerParams(
            collective_id=1, has_side_effects=True, vmem_limit_bytes=60 << 20
        ),
    )(
        features,
        features.reshape(span // EDGE, EDGE, width),
        adj_tiles.reshape(SLOTS, EDGE, EDGE),
        tile_rows.reshape(1, SLOTS),
        tile_cols.reshape(1, SLOTS),
        tile_count,
        w_neigh,
        w_self,
        bias.reshape(1, width),
        out_grad,
    )
    weight_grads = weight_grads.reshape(2, width, width)
    return act, grad_features, weight_grads[0], weight_grads[1], bias_grad[0]


def solution(mesh):
    spans = P(("blk", "rep"), None)
    in_specs = (
        spans,
        P("blk", "rep", None, None, None),
        P("blk", "rep", None),
        P("blk", "rep", None),
        P("blk", "rep"),
        P(),
        P(),
        P(),
        spans,
    )
    out_specs = (spans, spans, P(), P(), P())
    return jax.shard_map(local, mesh=mesh, in_specs=in_specs, out_specs=out_specs, check_vma=False)
```

time: 807 us -> 129 us (0.16)
  other arithmetic: 357 us -> 0 us
  matrix products: 124 us -> 0 us
  Pallas kernels: 0 us -> 120 us
  blocking collectives: 109 us -> 0 us
  waiting for transfers between devices: 103 us -> 0 us
  local copies, waits for them, and re-layouts: 95.7 us -> 6.46 us
  between operations: 14.6 us -> 1.29 us
    scatter-add x24 -> x0, other arithmetic: 318 us -> none  [the longest x8 156 us: backward_block(): return partial_back.at[cols_here].add(products * alive[:, None, None])]
    dot_general x22 -> x0, matrix products: 124 us -> none  [the longest x8 58.3 us: backward_block(): jnp.einsum('tij,tid->tjd', tile_block, picked, preferred_element_type=jnp...]
    pallas_call x0 -> x1, Pallas kernels: none -> 120 us  [local(): pl.pallas_call(layer_kernel, out_shape=(shaped((span, width), bf16), shap...]
    all_gather x2 -> x0, waiting for transfers between devices: 69.7 us -> none  [the longest x1 41.5 us: local(): lax.all_gather(features, 'rep', axis=0, tiled=True)]
    psum x1 -> x0, blocking collectives: 67.5 us -> none  [local(): lax.psum((neigh_local, self_local, bias_local), ('blk', 'rep'))]
    gather x16 -> x0, local copies, waits for them, and re-layouts: 62.5 us -> none  [the longest x8 39.6 us: forward_block(): picked = sources[cols_here]]
    unnamed x1 -> x0, blocking collectives: 41.3 us -> none
    reduce_scatter x2 -> x0, waiting for transfers between devices: 32.2 us -> none  [the longest x1 32.2 us: local(): lax.psum_scatter(partial_rounded.astype(jnp.bfloat16), 'blk', scatter_dim...]
  transfers between devices with their start and end apart: 5 -> 0, of which waited for: 3 -> 0; matrix products, arithmetic and copies ran while one was open for 35% -> 0% of each run, Pallas kernels for 0% -> 0%
where the time goes in v3:
time: 129 us; the launch traced here: 128 us
  Pallas kernels  120 us (93%)
  local copies, waits for them, and re-layouts  6.46 us (5%)
  between operations  1.29 us (1%)
    pallas_call x1, Pallas kernels, local(): pl.pallas_call(layer_kernel, out_shape=(shaped((span, width), bf16), shap...  120 us
    unnamed x2, local copies, waits for them, and re-layouts  3.34 us
    slice x2, local copies, waits for them, and re-layouts, local(): return (act, grad_features, weight_grads[0], weight_grads[1], bias_grad[0])  3.12 us

profile of v3, /device:TPU:2, one launch (start us, length us, event | category | flops | bytes accessed | tf_op | source)
XLA Modules:
  0.0 127.7 jit_solution(2251078545154058272)
XLA Ops:
  1.3 119.9 %shard_map.128 = (bf16[512,256]{1,0:T(8,128)(2,1)}, bf16[512,256]{1,0:T(8,128)(2,1)}, f32[16,32,256]{2,1,0:T(8,128)}, f32[8,256]{1,0:T(8,128)}) custom-call(bf16[512,256]{1,0:T(8,128)(2,1)} %features.1, bf16[4,128,256]{2,1,0:T(8,128)(2,1)} %bitcast.9, bf16[512,128,128]{2,1,0:T(8,128)(2,1)} %bitcast.8, s32[1,512]{1,0:T(1,128)} %bitcast.12, ...), custom_call_target="tpu_custom_call" | custom-call | tf_op jit(solution)/shard_map/pallas_call | solution.py:587
  121.2 1.3 slice.13
  122.5 1.9 %fusion = (f32[8,32,256]{2,1,0:T(8,128)}, f32[8,32,256]{2,1,0:T(8,128)}) fusion(f32[16,32,256]{2,1,0:T(8,128)} %get-tuple-element.11), kind=kLoop, calls=%fused_computation | loop fusion | bytes 1048576 | tf_op jit(solution)/shard_map/slice | solution.py:655
  124.3 1.7 %copy.17 = bf16[512,256]{1,0:T(8,128)(2,1)} copy(bf16[512,256]{1,0:T(8,128)(2,1)} %get-tuple-element.20) | data formatting | bytes 524288
  126.0 1.7 %copy.18 = bf16[512,256]{1,0:T(8,128)(2,1)} copy(bf16[512,256]{1,0:T(8,128)(2,1)} %get-tuple-element.21) | data formatting | bytes 524288

commit v4 on v3

--- a/solution.py
+++ b/solution.py
@@ -10,7 +10,7 @@
 MESH = pl.DeviceIdType.MESH
 EDGE = 128
 GROUP = 4
-UNROLL = 8
+BODIES = 8
 HALVES = 2
 SLOTS = 512
 ROW_TILES = 32
@@ -22,13 +22,13 @@
 f32, bf16, i32 = jnp.float32, jnp.bfloat16, jnp.int32
 
 
-def body_count(groups):
+def step_count(groups):
     steps = SLOTS // GROUP + groups * (GROUP - 1) // GROUP
-    return -(-steps // UNROLL)
-
-
-F_BODIES, B_BODIES = body_count(ROW_TILES), body_count(COL_TILES)
-STEPS = max(F_BODIES, B_BODIES) * UNROLL
+    return -(-steps // BODIES) * BODIES
+
+
+F_STEPS, B_STEPS = step_count(ROW_TILES), step_count(COL_TILES)
+STEPS = max(F_STEPS, B_STEPS)
 PLACES = -(-STEPS * GROUP // EDGE) * EDGE
 
 S_DEGREE = 0
@@ -40,7 +40,7 @@
 S_ALL = S_OUT + N_REP
 
 
-def write_plan(keys, others, live, plan, row, bodies):
+def write_plan(keys, others, live, plan, count):
     iota = lambda shape, axis: lax.broadcasted_iota(i32, shape, axis)
     square = (EDGE, EDGE)
     tall = (SLOTS, EDGE)
@@ -58,22 +58,22 @@
     before = (jnp.concatenate([key] * (SLOTS // EDGE), axis=1) == keys) & (iota(wide, 1) < iota(wide, 0))
     rank = count_of(before, 1)
     counts = count_of((key == lane) & alive, 0)
-    steps = (counts + (GROUP - 1)) // GROUP
+    steps = (counts + (GROUP - 1)) >> 2
     steps_down = stand(steps)
     base = jnp.sum(jnp.where(iota(square, 0) < iota(square, 1), steps_down, 0), axis=0, keepdims=True)
     base_down = stand(base)
     base_of = jnp.sum(jnp.where(key == lane, base, 0), axis=1, keepdims=True)
     place = jnp.where(alive, base_of * GROUP + rank, -1)
     code = slot * COL_TILES + other + 1
-    for c in range(-(-bodies * UNROLL * GROUP // EDGE)):
+    for c in range(-(-count * GROUP // EDGE)):
         here = pl.ds(c * EDGE, EDGE)
         found = jnp.sum(jnp.where(place == lane + c * EDGE, code, 0), axis=0, keepdims=True)
-        plan[row : row + 1, here] = jnp.where(found > 0, (found - 1) // COL_TILES, SLOTS)
-        plan[row + 1 : row + 2, here] = jnp.where(found > 0, (found - 1) % COL_TILES, 0)
-    for c in range(-(-bodies * UNROLL // EDGE)):
+        plan[0:1, here] = jnp.where(found > 0, (found - 1) >> 6, SLOTS)
+        plan[1:2, here] = jnp.where(found > 0, (found - 1) & (COL_TILES - 1), 0)
+    for c in range(-(-count // EDGE)):
         first = count_of((base_down == iota(square, 1) + c * EDGE) & (steps_down > 0), 0)
-        plan[row + 2 : row + 3, pl.ds(c * EDGE, EDGE)] = 1 - first
-    plan[row + 3 : row + 4, pl.ds(0, EDGE)] = jnp.where(steps > 0, base + steps - 1, -1)
+        plan[2:3, pl.ds(c * EDGE, EDGE)] = 1 - first
+    plan[3:4, pl.ds(0, EDGE)] = jnp.where(steps > 0, base + steps - 1, -1)
 
 
 class Links:
@@ -105,27 +105,28 @@
     buf, sources_0, sources_1, grads_0, grads_1, steps_out, total, degree_total, degree_steps,
     partial, degree, degrees, from_y, sums, to_x, from_x, own_grads, back, paired, arrivals,
     feats, out_grad, w_neigh, w_self, bias, mean, d_pre, self_term,
-    rep_out, rep_in, blk_out, blk_in, ints, plan, count, plan_s,
-    send_sems, recv_sems, load_sems, plan_sem,
+    rep_out, rep_in, blk_out, blk_in, ints, rows_plan, cols_plan, count, rows_plan_s, cols_plan_s,
+    send_sems, recv_sems, load_sems, plan_sems,
 ):
     blk, rep = lax.axis_index("blk"), lax.axis_index("rep")
-    y, x, z, core = blk // 2, (blk % 2) * 2 + rep // 8, (rep // 2) % 4, rep % 2
-    x_hi, x_lo = blk % 2, rep // 8
+    x_hi, x_lo = blk & 1, rep >> 3
+    y, x, z, core = blk >> 1, x_hi * 2 + x_lo, (rep >> 1) & 3, rep & 1
     sources, grads = (sources_0, sources_1), (grads_0, grads_1)
     links = Links(send_sems, recv_sems)
     piece_like = sources_0.at[pl.ds(0, 2)]
     chunk_like = sources_0.at[pl.ds(0, 4)]
+    rows_like = weight_grads.at[0, pl.ds(0, 32)]
 
     def device(dy=0, dx=0, dz=0, sibling=False, partner=False):
-        to_y, to_z = (y + dy) % 4, (z + dz) % 4
-        to_x = x + 1 - 2 * (x % 2) if partner else (x + dx) % 4
+        to_y, to_z = (y + dy) & 3, (z + dz) & 3
+        to_x = x ^ 1 if partner else (x + dx) & 3
         to_core = 1 - core if sibling else core
-        return (to_y * 2 + to_x // 2, (to_x % 2) * 8 + to_z * 2 + to_core)
+        return (to_y * 2 + (to_x >> 1), (to_x & 1) * 8 + to_z * 2 + to_core)
 
     y_up, y_down, z_up, z_down = device(dy=1), device(dy=-1), device(dz=1), device(dz=-1)
     across, sibling, far_x = device(partner=True), device(sibling=True), device(dx=2)
-    blk_peer = lambda d: ((blk + d) % N_BLK, rep)
-    rep_peer = lambda d: (blk, (rep + d) % N_REP)
+    blk_peer = lambda d: ((blk + d) & (N_BLK - 1), rep)
+    rep_peer = lambda d: (blk, (rep + d) & (N_REP - 1))
 
     loads = []
 
@@ -152,7 +153,7 @@
     pl.semaphore_wait(barrier, len(peers))
 
     def rep_block(dx, dz, half, other_core=False):
-        index = ((x_lo + dx) % 2) * 8 + ((z + dz) % 4) * 2 + (1 - core if other_core else core)
+        index = ((x_lo + dx) & 1) * 8 + ((z + dz) & 3) * 2 + (1 - core if other_core else core)
         return pl.ds(index * 4 + 2 * half, 2)
 
     def sem(h, run, k):
@@ -206,59 +207,76 @@
         copy.wait()
     gather_start(0, 0, 1, 2, 3, 4, 5)
     gather_sibling(0)
-    gather_start(1, 0, 1, 2, 3)
 
     for copy in int_loads:
         copy.wait()
     live = count[0, 0]
     row_keys, col_keys = ints[0:1], ints[1:2]
-    write_plan(row_keys, col_keys, live, plan, 0, F_BODIES)
-    gather(0, 2, 3, 0, 1)
-    gather_start(1, 4, 5)
-    gather_sibling(1)
-    write_plan(col_keys, row_keys, live, plan, 4, B_BODIES)
-    plan_copy = pltpu.make_async_copy(plan, plan_s, plan_sem)
-    plan_copy.start()
+
+    def write_and_move(keys, others, plan, plan_s, steps, n):
+        write_plan(keys, others, live, plan, steps)
+        copy = pltpu.make_async_copy(plan, plan_s, plan_sems.at[n])
+        copy.start()
+        return copy
+
+    write_and_move(row_keys, col_keys, rows_plan, rows_plan_s, F_STEPS, 0).wait()
     buf[SLOTS] = jnp.zeros((EDGE, EDGE), bf16)
-    gather(0, 4, 5)
-    gather(1, 2, 3)
-    gather(0, 8, 9)
-    gather(1, 0, 1)
-    gather(0, 6, 7, 10, 11)
-    gather(1, 4, 5)
-    gather(0, 12, 13)
     for copy in tile_loads:
         copy.wait()
-    plan_copy.wait()
+    ones = jnp.ones((16, EDGE), bf16)
+    degree_total[...] = jnp.zeros_like(degree_total)
+
+    @pl.loop(0, F_STEPS // 8)
+    def _(body):
+        value = degree_total[...]
+        for k in range(8):
+            n = body * 8 + k
+            held = [buf[rows_plan_s[0, n * GROUP + m]] for m in range(GROUP)]
+            marks = (held[0] + held[1]) + (held[2] + held[3])
+            here = lax.dot_general(ones, marks, OVER_COLS, preferred_element_type=f32)
+            value = value * rows_plan_s[2, n].astype(f32) + here[0:8]
+            degree_steps[n] = value
+        degree_total[...] = value
+        pl.when(body == 8)(lambda: gather(0, 2, 3, 0, 1))
+        pl.when(body == 14)(lambda: gather(0, 4, 5))
+
+    cols_copy = write_and_move(col_keys, row_keys, cols_plan, cols_plan_s, B_STEPS, 1)
+    gather(0, 8, 9)
+    gather_start(1, 0, 1, 2, 3, 4, 5)
+    gather_sibling(1)
+
+    @pl.loop(0, ROW_TILES)
+    def _(n):
+        at = rows_plan_s[3, n]
+        degree[n] = degree_steps[jnp.maximum(at, 0)] * jnp.where(at >= 0, 1.0, 0.0)
+
+    gather(0, 6, 7, 10, 11, 12, 13)
+    cols_copy.wait()
     gather_end(0)
 
-    def tile_pass(row, bodies, product, extra=None, hooks=()):
+    def tile_pass(plan_s, steps, product, hooks=()):
         total[...] = jnp.zeros_like(total)
 
-        @pl.loop(0, bodies)
+        @pl.loop(0, BODIES)
         def _(body):
             value = total[...]
-            for k in range(UNROLL):
-                n = body * UNROLL + k
+            for k in range(steps // BODIES):
+                n = body * (steps // BODIES) + k
                 places = [n * GROUP + m for m in range(GROUP)]
-                held = [buf[plan_s[row, p]] for p in places]
-                keep = plan_s[row + 2, n].astype(f32)
-                value = value * keep + product(held, [plan_s[row + 1, p] for p in places])
+                held = [buf[plan_s[0, p]] for p in places]
+                keep = plan_s[2, n].astype(f32)
+                value = value * keep + product(held, [plan_s[1, p] for p in places])
                 steps_out[n] = value.astype(bf16)
-                if extra is not None:
-                    extra(n, keep, held)
             total[...] = value
             for when, action in hooks:
-                pl.when(body == when)(action)
-
-    def collect(row, count, target):
+                pl.when(body == (when + 1) * BODIES // 8 - 1)(action)
+
+    def collect(plan_s, count, target):
         @pl.loop(0, count)
         def _(n):
-            at = plan_s[row + 3, n]
+            at = plan_s[3, n]
             has = jnp.where(at >= 0, 1.0, 0.0)
             target[n] = (steps_out[jnp.maximum(at, 0)].astype(f32) * has).astype(bf16)
-
-    ones = jnp.ones((16, EDGE), bf16)
 
     def forward(h):
         def product(held, others):
@@ -268,30 +286,19 @@
 
         return product
 
-    def row_sums(n, keep, held):
-        marks = (held[0] + held[1]) + (held[2] + held[3])
-        sums_here = lax.dot_general(ones, marks, OVER_COLS, preferred_element_type=f32)[0:8]
-        degree_total[...] = degree_total[...] * keep + sums_here
-        degree_steps[n] = degree_total[...]
-
-    degree_total[...] = jnp.zeros_like(degree_total)
     tile_pass(
-        0, F_BODIES, forward(0), row_sums,
+        rows_plan_s, F_STEPS, forward(0),
         hooks=(
+            (1, lambda: gather(1, 2, 3, 0, 1)),
+            (2, lambda: gather(1, 4, 5)),
             (4, lambda: gather(1, 8, 9)),
-            (9, lambda: gather(1, 6, 7, 10, 11)),
-            (14, lambda: gather(1, 12, 13)),
+            (6, lambda: gather(1, 6, 7, 10)),
         ),
     )
-    collect(0, ROW_TILES, partial.at[0])
-
-    @pl.loop(0, ROW_TILES)
-    def _(n):
-        at = plan_s[3, n]
-        degree[n] = degree_steps[jnp.maximum(at, 0)] * jnp.where(at >= 0, 1.0, 0.0)
+    collect(rows_plan_s, ROW_TILES, partial.at[0])
 
     def blk_block(dy, j):
-        return ((y + dy) % 4) * 2 + (x_hi if j else 1 - x_hi)
+        return ((y + dy) & 3) * 2 + (x_hi if j else 1 - x_hi)
 
     def part(h, dy, j, half):
         return partial.at[h, pl.ds(blk_block(dy, j) * 4 + 2 * half, 2)]
@@ -326,27 +333,31 @@
             to_x[h, 2 * half : 2 * half + 2] = sum_y(h, 0, half).astype(bf16)
         links.send(sem(h, S_SUM, 12), to_x.at[h], from_x.at[h], far_x, chunk_like)
 
-    sum_far(0, 0)
-    sum_far(0, 1)
-    sum_near(0, 0)
-    for d in range(1, N_BLK):
-        to = (blk + d) % N_BLK
-        links.send(S_DEGREE + d, degree.at[pl.ds(to * 4, 4)], degrees.at[d], blk_peer(d), degrees.at[0])
-    gather_end(1)
+    def sum_start(h):
+        sum_far(h, 0)
+        sum_near(h, 0)
 
     def sum_middle(h):
         sum_combine(h, 0)
+        sum_far(h, 1)
         sum_near(h, 1)
 
+    sum_start(0)
+    for d in range(1, N_BLK):
+        to = (blk + d) & (N_BLK - 1)
+        links.send(S_DEGREE + d, degree.at[pl.ds(to * 4, 4)], degrees.at[d], blk_peer(d), degrees.at[0])
+    gather(1, 11, 12, 13)
+    gather_end(1)
     tile_pass(
-        0, F_BODIES, forward(1),
-        hooks=((10, lambda: sum_middle(0)), (14, lambda: sum_combine(0, 1))),
+        rows_plan_s, F_STEPS, forward(1),
+        hooks=(
+            (2, lambda: sum_middle(0)),
+            (6, lambda: sum_across(0)),
+            (7, lambda: sum_combine(0, 1)),
+        ),
     )
-    collect(0, ROW_TILES, partial.at[1])
-    sum_far(1, 0)
-    sum_far(1, 1)
-    sum_near(1, 0)
-    sum_across(0)
+    collect(rows_plan_s, ROW_TILES, partial.at[1])
+    sum_start(1)
     sum_middle(1)
     sum_combine(1, 1)
     for copy in node_loads:
@@ -428,46 +439,48 @@
     neigh = lax.dot_general(mean[...], d_pre[...], OVER_ROWS, preferred_element_type=f32)
     for p in range(8):
         rep_out[p, 0:32] = neigh[32 * p : 32 * p + 32].astype(bf16)
-    grads_onward(0, 1)
-    grads_along(1, 1)
     own = lax.dot_general(feats[...], d_pre[...], OVER_ROWS, preferred_element_type=f32)
     for p in range(8):
         rep_out[8 + p, 0:32] = own[32 * p : 32 * p + 32].astype(bf16)
+    grads_onward(0, 1)
     own_bias = two_rows(jnp.sum(d_pre[...].astype(f32), axis=0, keepdims=True))
     for p in range(N_REP):
         rep_out[p, 32:48] = own_bias
     for d in range(1, N_REP):
-        links.send(S_REP + d, rep_out.at[(rep + d) % N_REP], rep_in.at[d], rep_peer(d), rep_in.at[0])
+        links.send(S_REP + d, rep_out.at[(rep + d) & (N_REP - 1)], rep_in.at[d], rep_peer(d), rep_in.at[0])
     rep_in[0] = rep_out[rep]
     grads_other(0)
-    grads_onward(1, 1)
     self_term[...] = lax.dot_general(d_pre[...], w_self[...], OVER_COLS, preferred_element_type=f32)
 
     for d in range(1, N_REP):
         links.arrived(S_REP + d, rep_in.at[d])
     summed = rep_in[rep].astype(f32)
     for source in range(1, N_REP):
-        summed += rep_in[(rep + N_REP - source) % N_REP].astype(f32)
+        summed += rep_in[(rep - source) & (N_REP - 1)].astype(f32)
     blk_out[0:32] = summed[0:32].astype(bf16)
     blk_out[32:48] = two_rows(summed[32:33] + summed[33:34])
+    grads_onward(0, 0)
+    grads_along(1, 1)
     for d in range(1, N_BLK):
         links.send(S_BLK + d, blk_out, blk_in.at[d], blk_peer(d), blk_in.at[0])
     blk_in[0] = blk_out[...]
-    grads_onward(0, 0)
-    grads_other(1)
+
+    def own_weights(d=0):
+        index = (rep - d) & (N_REP - 1)
+        return weight_grads.at[index // 8, pl.ds((index & 7) * 32, 32)]
 
     def weights_end():
         for d in range(1, N_BLK):
             links.arrived(S_BLK + d, blk_in.at[d])
         summed = blk_in[blk].astype(f32)
         for source in range(1, N_BLK):
-            summed += blk_in[(blk + N_BLK - source) % N_BLK].astype(f32)
-        weight_grads[rep] = summed[0:32]
+            summed += blk_in[(blk - source) & (N_BLK - 1)].astype(f32)
+        mine = own_weights()
+        mine[...] = summed[0:32]
         bias_grad[...] = jnp.broadcast_to(summed[32:33] + summed[33:34], bias_grad.shape)
         for d in range(1, N_REP):
-            links.send(S_OUT + d, weight_grads.at[rep], weight_grads.at[rep], rep_peer(d), weight_grads.at[0])
-
-    weights_end()
+            links.send(S_OUT + d, mine, mine, rep_peer(d), rows_like)
+
     grads_end(0)
 
     def backward(h):
@@ -478,13 +491,21 @@
 
         return product
 
-    tile_pass(4, B_BODIES, backward(0), hooks=((2, lambda: grads_onward(1, 0)),))
-    collect(4, COL_TILES, back.at[0])
+    tile_pass(
+        cols_plan_s, B_STEPS, backward(0),
+        hooks=(
+            (0, lambda: grads_other(1)),
+            (1, lambda: grads_onward(1, 1)),
+            (2, weights_end),
+            (4, lambda: grads_onward(1, 0)),
+        ),
+    )
+    collect(cols_plan_s, COL_TILES, back.at[0])
 
     order = ((1, 2), (1, 1), (1, -1), (0, 2), (0, 1), (0, -1), (1, 0), (0, 0))
 
     def back_block(dx, dz, other_core):
-        index = ((x_lo + dx) % 2) * 8 + ((z + dz) % 4) * 2 + (1 - core if other_core else core)
+        index = ((x_lo + dx) & 1) * 8 + ((z + dz) & 3) * 2 + (1 - core if other_core else core)
         return pl.ds(index * 4, 4)
 
     def back_start(h):
@@ -559,14 +580,14 @@
     back_raw(0)
     grads_end(1)
     tile_pass(
-        4, B_BODIES, backward(1),
+        cols_plan_s, B_STEPS, backward(1),
         hooks=(
-            (8, lambda: back_first(0)),
-            (12, lambda: back_second(0)),
-            (18, lambda: back_third(0)),
+            (3, lambda: back_first(0)),
+            (4, lambda: back_second(0)),
+            (6, lambda: back_third(0)),
         ),
     )
-    collect(4, COL_TILES, back.at[1])
+    collect(cols_plan_s, COL_TILES, back.at[1])
     back_raw(1)
     back_first(1)
     back_second(1)
@@ -574,8 +595,27 @@
     back_end(0)
     back_end(1)
     for d in range(1, N_REP):
-        links.arrived(S_OUT + d, weight_grads.at[(rep + N_REP - d) % N_REP])
+        links.arrived(S_OUT + d, own_weights(d))
     links.drain()
+
+
+def write_kernel(act, grad_features, weight_grads, bias_grad, act_to, grad_to, neigh_to, own_to, bias_to, rows, square, line, sems):
+    ways = (
+        (act, rows.at[0], act_to),
+        (grad_features, rows.at[1], grad_to),
+        (weight_grads.at[0], square.at[0], neigh_to),
+        (weight_grads.at[1], square.at[1], own_to),
+        (bias_grad.at[pl.ds(0, 1)], line, bias_to),
+    )
+    first = [pltpu.make_async_copy(source, held, sems.at[0, n]) for n, (source, held, _) in enumerate(ways)]
+    second = [pltpu.make_async_copy(held, target, sems.at[1, n]) for n, (_, held, target) in enumerate(ways)]
+    for copy in first:
+        copy.start()
+    for done, copy in zip(first, second):
+        done.wait()
+        copy.start()
+    for copy in second:
+        copy.wait()
 
 
 def local(features, adj_tiles, tile_rows, tile_cols, tile_count, w_neigh, w_self, bias, out_grad):
@@ -589,7 +629,7 @@
         out_shape=(
             shaped((span, width), bf16),
             shaped((span, width), bf16),
-            shaped((N_REP, 32, width), f32),
+            shaped((2, width, width), f32),
             shaped((8, width), f32),
         ),
         in_specs=[any_spec] * 10,
@@ -603,7 +643,7 @@
             VMEM((STEPS, *square), bf16),
             VMEM(square, f32),
             VMEM((8, EDGE), f32),
-            VMEM((F_BODIES * UNROLL, 8, EDGE), f32),
+            VMEM((F_STEPS, 8, EDGE), f32),
             VMEM((HALVES, ROW_TILES, *square), bf16),
             VMEM((ROW_TILES, 8, EDGE), f32),
             VMEM((N_BLK, 4, 8, EDGE), f32),
@@ -629,12 +669,14 @@
             VMEM((N_BLK, 48, width), bf16),
             VMEM((8, SLOTS), i32),
             VMEM((8, PLACES), i32),
+            VMEM((8, PLACES), i32),
             pltpu.SMEM((1, 1), i32),
+            pltpu.SMEM((8, PLACES), i32),
             pltpu.SMEM((8, PLACES), i32),
             pltpu.SemaphoreType.DMA((S_ALL,)),
             pltpu.SemaphoreType.DMA((S_ALL,)),
             pltpu.SemaphoreType.DMA((18,)),
-            pltpu.SemaphoreType.DMA,
+            pltpu.SemaphoreType.DMA((2,)),
         ],
         compiler_params=pltpu.CompilerParams(
             collective_id=1, has_side_effects=True, vmem_limit_bytes=60 << 20
@@ -651,8 +693,26 @@
         bias.reshape(1, width),
         out_grad,
     )
-    weight_grads = weight_grads.reshape(2, width, width)
-    return act, grad_features, weight_grads[0], weight_grads[1], bias_grad[0]
+    results = pl.pallas_call(
+        write_kernel,
+        out_shape=(
+            shaped((span, width), bf16),
+            shaped((span, width), bf16),
+            shaped((width, width), f32),
+            shaped((width, width), f32),
+            shaped((1, width), f32),
+        ),
+        in_specs=[any_spec] * 4,
+        out_specs=(any_spec,) * 5,
+        scratch_shapes=[
+            VMEM((2, span, width), bf16),
+            VMEM((2, width, width), f32),
+            VMEM((1, width), f32),
+            pltpu.SemaphoreType.DMA((2, 5)),
+        ],
+        compiler_params=pltpu.CompilerParams(vmem_limit_bytes=60 << 20),
+    )(act, grad_features, weight_grads, bias_grad)
+    return (*results[:4], results[4].reshape(width))
 
 
 def solution(mesh):

time: 129 us -> 120 us (0.930)
  local copies, waits for them, and re-layouts: 6.46 us -> 0 us
    pallas_call x1, Pallas kernels: 120 us -> 117 us  [local(): pl.pallas_call(layer_kernel, out_shape=(shaped((span, width), bf16), shap...]
    unnamed x2 -> x0, local copies, waits for them, and re-layouts: 3.34 us -> none
    slice x2 -> x0, local copies, waits for them, and re-layouts: 3.12 us -> none  [local(): return (act, grad_features, weight_grads[0], weight_grads[1], bias_grad[0])]
    pallas_call x0 -> x1, Pallas kernels: none -> 2 us  [local(): pl.pallas_call(write_kernel, out_shape=(shaped((span, width), bf16), shap...]
where the time goes in v4:
time: 120 us
  Pallas kernels  119 us (99%)
  between operations  1.29 us (1%)
    pallas_call x1, Pallas kernels, local(): pl.pallas_call(layer_kernel, out_shape=(shaped((span, width), bf16), shap...  117 us

profile of v4, /device:TPU:2, one launch (start us, length us, event | category | flops | bytes accessed | tf_op | source)
XLA Modules:
  0.0 119.8 jit_solution(14265616493918345047)
XLA Ops:
  1.3 116.5 %shard_map.128 = (bf16[512,256]{1,0:T(8,128)(2,1)}, bf16[512,256]{1,0:T(8,128)(2,1)}, f32[2,256,256]{2,1,0:T(8,128)}, f32[8,256]{1,0:T(8,128)}) custom-call(bf16[512,256]{1,0:T(8,128)(2,1)} %features.1, bf16[4,128,256]{2,1,0:T(8,128)(2,1)} %bitcast.7, bf16[512,128,128]{2,1,0:T(8,128)(2,1)} %bitcast.6, s32[1,512]{1,0:T(1,128)} %bitcast.8, s32[1,512]{1,0:T(1,128)} %bitcast.9, ...), custom_call_target="tpu_custom_call" | custom-call | tf_op jit(solution)/shard_map/pallas_call | solution.py:627
  117.8 2.0 %shard_map.129 = (bf16[512,256]{1,0:T(8,128)(2,1)}, bf16[512,256]{1,0:T(8,128)(2,1)}, f32[256,256]{1,0:T(8,128)}, f32[256,256]{1,0:T(8,128)}, f32[1,256]{1,0:T(1,128)}) custom-call(bf16[512,256]{1,0:T(8,128)(2,1)} %get-tuple-element.14.act, bf16[512,256]{1,0:T(8,128)(2,1)} %get-tuple-element.15.grad_features, f32[2,256,256]{2,1,0:T(8,128)} %get-tuple-element.16.weight_grads, ...), custom_call_target="tpu_custom_call" | custom-call | tf_op jit(solution)/shard_map/pallas_call | solution.py:696

commit v5 on v4

--- a/solution.py
+++ b/solution.py
@@ -17,6 +17,7 @@
 COL_TILES = 64
 N_BLK = 8
 N_REP = 16
+N_CHIPS = 8
 OVER_ROWS = (((0,), (0,)), ((), ()))
 OVER_COLS = (((1,), (1,)), ((), ()))
 f32, bf16, i32 = jnp.float32, jnp.bfloat16, jnp.int32
@@ -35,9 +36,9 @@
 S_GATHER, S_SUM, S_GRADS, S_BACK, S_HALF = 0, 30, 43, 56, 78
 S_FIRST = 8
 S_REP = S_FIRST + HALVES * S_HALF
-S_BLK = S_REP + N_REP
+S_BLK = S_REP + N_CHIPS
 S_OUT = S_BLK + N_BLK
-S_ALL = S_OUT + N_REP
+S_ALL = S_OUT + N_CHIPS
 
 
 def write_plan(keys, others, live, plan, count):
@@ -105,7 +106,7 @@
     buf, sources_0, sources_1, grads_0, grads_1, steps_out, total, degree_total, degree_steps,
     partial, degree, degrees, from_y, sums, to_x, from_x, own_grads, back, paired, arrivals,
     feats, out_grad, w_neigh, w_self, bias, mean, d_pre, self_term,
-    rep_out, rep_in, blk_out, blk_in, ints, rows_plan, cols_plan, count, rows_plan_s, cols_plan_s,
+    rep_out, pair_in, rep_sum, rep_in, blk_out, blk_in, ints, rows_plan, cols_plan, count, rows_plan_s, cols_plan_s,
     send_sems, recv_sems, load_sems, plan_sems,
 ):
     blk, rep = lax.axis_index("blk"), lax.axis_index("rep")
@@ -115,6 +116,7 @@
     links = Links(send_sems, recv_sems)
     piece_like = sources_0.at[pl.ds(0, 2)]
     chunk_like = sources_0.at[pl.ds(0, 4)]
+    matrix_like = weight_grads.at[0]
     rows_like = weight_grads.at[0, pl.ds(0, 32)]
 
     def device(dy=0, dx=0, dz=0, sibling=False, partner=False):
@@ -126,7 +128,8 @@
     y_up, y_down, z_up, z_down = device(dy=1), device(dy=-1), device(dz=1), device(dz=-1)
     across, sibling, far_x = device(partner=True), device(sibling=True), device(dx=2)
     blk_peer = lambda d: ((blk + d) & (N_BLK - 1), rep)
-    rep_peer = lambda d: (blk, (rep + d) & (N_REP - 1))
+    chip = rep >> 1
+    chip_peer = lambda d: (blk, ((chip + d) & (N_CHIPS - 1)) * 2 + core)
 
     loads = []
 
@@ -147,7 +150,7 @@
     ]
 
     barrier = pltpu.get_barrier_semaphore()
-    peers = [far_x] + [blk_peer(d) for d in range(1, N_BLK)] + [rep_peer(d) for d in range(1, N_REP)]
+    peers = [sibling] + [chip_peer(d) for d in range(1, N_CHIPS)] + [blk_peer(d) for d in range(1, N_BLK)]
     for peer in peers:
         pl.semaphore_signal(barrier, inc=1, device_id=peer, device_id_type=MESH)
     pl.semaphore_wait(barrier, len(peers))
@@ -219,10 +222,17 @@
         copy.start()
         return copy
 
-    write_and_move(row_keys, col_keys, rows_plan, rows_plan_s, F_STEPS, 0).wait()
+    rows_copy = write_and_move(row_keys, col_keys, rows_plan, rows_plan_s, F_STEPS, 0)
+    cols_copy = write_and_move(col_keys, row_keys, cols_plan, cols_plan_s, B_STEPS, 1)
     buf[SLOTS] = jnp.zeros((EDGE, EDGE), bf16)
+    rows_copy.wait()
+    cols_copy.wait()
+    gather(0, 2, 3, 0, 1, 4, 5)
     for copy in tile_loads:
         copy.wait()
+    gather(0, 8, 9)
+    gather_start(1, 0, 1, 2, 3, 4, 5)
+    gather_sibling(1)
     ones = jnp.ones((16, EDGE), bf16)
     degree_total[...] = jnp.zeros_like(degree_total)
 
@@ -237,21 +247,9 @@
             value = value * rows_plan_s[2, n].astype(f32) + here[0:8]
             degree_steps[n] = value
         degree_total[...] = value
-        pl.when(body == 8)(lambda: gather(0, 2, 3, 0, 1))
-        pl.when(body == 14)(lambda: gather(0, 4, 5))
-
-    cols_copy = write_and_move(col_keys, row_keys, cols_plan, cols_plan_s, B_STEPS, 1)
-    gather(0, 8, 9)
-    gather_start(1, 0, 1, 2, 3, 4, 5)
-    gather_sibling(1)
-
-    @pl.loop(0, ROW_TILES)
-    def _(n):
-        at = rows_plan_s[3, n]
-        degree[n] = degree_steps[jnp.maximum(at, 0)] * jnp.where(at >= 0, 1.0, 0.0)
-
-    gather(0, 6, 7, 10, 11, 12, 13)
-    cols_copy.wait()
+        pl.when(body == 6)(lambda: gather(0, 6, 7, 10, 11))
+        pl.when(body == 16)(lambda: gather(0, 12, 13))
+
     gather_end(0)
 
     def tile_pass(plan_s, steps, product, hooks=()):
@@ -343,6 +341,12 @@
         sum_near(h, 1)
 
     sum_start(0)
+
+    @pl.loop(0, ROW_TILES)
+    def _(n):
+        at = rows_plan_s[3, n]
+        degree[n] = degree_steps[jnp.maximum(at, 0)] * jnp.where(at >= 0, 1.0, 0.0)
+
     for d in range(1, N_BLK):
         to = (blk + d) & (N_BLK - 1)
         links.send(S_DEGREE + d, degree.at[pl.ds(to * 4, 4)], degrees.at[d], blk_peer(d), degrees.at[0])
@@ -437,37 +441,45 @@
         return jnp.where(which == 0, high, jnp.where(which == 1, v - high, 0.0)).astype(bf16)
 
     neigh = lax.dot_general(mean[...], d_pre[...], OVER_ROWS, preferred_element_type=f32)
-    for p in range(8):
-        rep_out[p, 0:32] = neigh[32 * p : 32 * p + 32].astype(bf16)
+    for p in range(N_CHIPS):
+        rep_out[0, p, 0:32] = neigh[32 * p : 32 * p + 32].astype(bf16)
     own = lax.dot_general(feats[...], d_pre[...], OVER_ROWS, preferred_element_type=f32)
-    for p in range(8):
-        rep_out[8 + p, 0:32] = own[32 * p : 32 * p + 32].astype(bf16)
+    for p in range(N_CHIPS):
+        rep_out[1, p, 0:32] = own[32 * p : 32 * p + 32].astype(bf16)
+    own_bias = two_rows(jnp.sum(d_pre[...].astype(f32), axis=0, keepdims=True))
+    for c in range(2):
+        for p in range(N_CHIPS):
+            rep_out[c, p, 32:48] = own_bias
+    links.send(S_REP, rep_out.at[1 - core], pair_in, sibling, pair_in)
     grads_onward(0, 1)
-    own_bias = two_rows(jnp.sum(d_pre[...].astype(f32), axis=0, keepdims=True))
-    for p in range(N_REP):
-        rep_out[p, 32:48] = own_bias
-    for d in range(1, N_REP):
-        links.send(S_REP + d, rep_out.at[(rep + d) & (N_REP - 1)], rep_in.at[d], rep_peer(d), rep_in.at[0])
-    rep_in[0] = rep_out[rep]
+    links.arrived(S_REP, pair_in)
+    for p in range(N_CHIPS):
+        mine, other = rep_out[core, p].astype(f32), pair_in[p].astype(f32)
+        rep_sum[p, 0:32] = (mine[0:32] + other[0:32]).astype(bf16)
+        if p == 0:
+            pair_bias = two_rows((mine[32:33] + mine[33:34]) + (other[32:33] + other[33:34]))
+        rep_sum[p, 32:48] = pair_bias
+    for d in range(1, N_CHIPS):
+        links.send(S_REP + d, rep_sum.at[(chip + d) & (N_CHIPS - 1)], rep_in.at[d], chip_peer(d), rep_in.at[0])
+    rep_in[0] = rep_sum[chip]
     grads_other(0)
     self_term[...] = lax.dot_general(d_pre[...], w_self[...], OVER_COLS, preferred_element_type=f32)
 
-    for d in range(1, N_REP):
+    for d in range(1, N_CHIPS):
         links.arrived(S_REP + d, rep_in.at[d])
-    summed = rep_in[rep].astype(f32)
-    for source in range(1, N_REP):
-        summed += rep_in[(rep - source) & (N_REP - 1)].astype(f32)
+    summed = rep_in[chip].astype(f32)
+    for source in range(1, N_CHIPS):
+        summed += rep_in[(chip - source) & (N_CHIPS - 1)].astype(f32)
     blk_out[0:32] = summed[0:32].astype(bf16)
     blk_out[32:48] = two_rows(summed[32:33] + summed[33:34])
     grads_onward(0, 0)
-    grads_along(1, 1)
     for d in range(1, N_BLK):
         links.send(S_BLK + d, blk_out, blk_in.at[d], blk_peer(d), blk_in.at[0])
     blk_in[0] = blk_out[...]
+    grads_along(1, 1)
 
     def own_weights(d=0):
-        index = (rep - d) & (N_REP - 1)
-        return weight_grads.at[index // 8, pl.ds((index & 7) * 32, 32)]
+        return weight_grads.at[core, pl.ds(((chip - d) & (N_CHIPS - 1)) * 32, 32)]
 
     def weights_end():
         for d in range(1, N_BLK):
@@ -478,8 +490,13 @@
         mine = own_weights()
         mine[...] = summed[0:32]
         bias_grad[...] = jnp.broadcast_to(summed[32:33] + summed[33:34], bias_grad.shape)
-        for d in range(1, N_REP):
-            links.send(S_OUT + d, mine, mine, rep_peer(d), rows_like)
+        for d in range(1, N_CHIPS):
+            links.send(S_OUT + d, mine, mine, chip_peer(d), rows_like)
+
+    def weights_share():
+        for d in range(1, N_CHIPS):
+            links.arrived(S_OUT + d, own_weights(d))
+        links.send(S_OUT, weight_grads.at[core], weight_grads.at[core], sibling, matrix_like)
 
     grads_end(0)
 
@@ -531,7 +548,6 @@
         ref[...] = (ref[...].astype(f32) + arrivals[h, k].astype(f32)).astype(bf16)
 
     def back_raw(h):
-        back_start(h)
         back_pair(h, 1, 2)
         back_send(h, 0, 1, 2, 0, z_down)
         back_send(h, 1, 1, 2, 1, z_up)
@@ -542,6 +558,8 @@
         back_pair(h, 0, 2)
         back_send(h, 4, 0, 2, 0, z_down)
         back_send(h, 5, 0, 2, 1, z_up)
+
+    def back_pairs(h):
         for dx, dz in order[4:]:
             back_pair(h, dx, dz)
 
@@ -577,25 +595,29 @@
                 here, lanes = pl.ds((2 * half + t) * EDGE, EDGE), pl.ds(h * EDGE, EDGE)
                 grad_features[here, lanes] = (self_term[here, lanes] + jnp.transpose(value[t])).astype(bf16)
 
-    back_raw(0)
+    back_start(0)
     grads_end(1)
     tile_pass(
         cols_plan_s, B_STEPS, backward(1),
         hooks=(
-            (3, lambda: back_first(0)),
-            (4, lambda: back_second(0)),
-            (6, lambda: back_third(0)),
+            (0, lambda: back_raw(0)),
+            (2, lambda: back_pairs(0)),
+            (4, lambda: back_first(0)),
+            (5, lambda: back_second(0)),
+            (6, weights_share),
         ),
     )
     collect(cols_plan_s, COL_TILES, back.at[1])
+    back_start(1)
+    back_third(0)
     back_raw(1)
+    back_pairs(1)
     back_first(1)
     back_second(1)
+    back_end(0)
     back_third(1)
-    back_end(0)
     back_end(1)
-    for d in range(1, N_REP):
-        links.arrived(S_OUT + d, own_weights(d))
+    links.arrived(S_OUT, weight_grads.at[1 - core])
     links.drain()
 
 
@@ -663,8 +685,10 @@
             VMEM((span, width), bf16),
             VMEM((span, width), bf16),
             VMEM((span, width), f32),
-            VMEM((N_REP, 48, width), bf16),
-            VMEM((N_REP, 48, width), bf16),
+            VMEM((2, N_CHIPS, 48, width), bf16),
+            VMEM((N_CHIPS, 48, width), bf16),
+            VMEM((N_CHIPS, 48, width), bf16),
+            VMEM((N_CHIPS, 48, width), bf16),
             VMEM((48, width), bf16),
             VMEM((N_BLK, 48, width), bf16),
             VMEM((8, SLOTS), i32),

time: 120 us -> 114 us (0.950)
  Pallas kernels: 119 us -> 111 us
    pallas_call x1, Pallas kernels: 117 us -> 109 us  [local(): pl.pallas_call(layer_kernel, out_shape=(shaped((span, width), bf16), shap...]
where the time goes in v5:
time: 114 us; the launch traced here: 113 us
  Pallas kernels  111 us (97%)
  between operations  1.29 us (1%)
    pallas_call x1, Pallas kernels, local(): pl.pallas_call(layer_kernel, out_shape=(shaped((span, width), bf16), shap...  109 us

profile of v5, /device:TPU:2, one launch (start us, length us, event | category | flops | bytes accessed | tf_op | source)
XLA Modules:
  0.0 112.7 jit_solution(1187024223922502016)
XLA Ops:
  1.3 109.4 %shard_map.128 = (bf16[512,256]{1,0:T(8,128)(2,1)}, bf16[512,256]{1,0:T(8,128)(2,1)}, f32[2,256,256]{2,1,0:T(8,128)}, f32[8,256]{1,0:T(8,128)}) custom-call(bf16[512,256]{1,0:T(8,128)(2,1)} %features.1, bf16[4,128,256]{2,1,0:T(8,128)(2,1)} %bitcast.7, bf16[512,128,128]{2,1,0:T(8,128)(2,1)} %bitcast.6, s32[1,512]{1,0:T(1,128)} %bitcast.8, s32[1,512]{1,0:T(1,128)} %bitcast.9, ...), custom_call_target="tpu_custom_call" | custom-call | tf_op jit(solution)/shard_map/pallas_call | solution.py:649
  110.7 2.0 %shard_map.129 = (bf16[512,256]{1,0:T(8,128)(2,1)}, bf16[512,256]{1,0:T(8,128)(2,1)}, f32[256,256]{1,0:T(8,128)}, f32[256,256]{1,0:T(8,128)}, f32[1,256]{1,0:T(1,128)}) custom-call(bf16[512,256]{1,0:T(8,128)(2,1)} %get-tuple-element.14.act, bf16[512,256]{1,0:T(8,128)(2,1)} %get-tuple-element.15.grad_features, f32[2,256,256]{2,1,0:T(8,128)} %get-tuple-element.16.weight_grads, ...), custom_call_target="tpu_custom_call" | custom-call | tf_op jit(solution)/shard_map/pallas_call | solution.py:720

commit v6 on v5

--- a/solution.py
+++ b/solution.py
@@ -11,6 +11,7 @@
 EDGE = 128
 GROUP = 4
 BODIES = 8
+DEGREE_MIDDLE = 9
 HALVES = 2
 SLOTS = 512
 ROW_TILES = 32
@@ -233,23 +234,7 @@
     gather(0, 8, 9)
     gather_start(1, 0, 1, 2, 3, 4, 5)
     gather_sibling(1)
-    ones = jnp.ones((16, EDGE), bf16)
-    degree_total[...] = jnp.zeros_like(degree_total)
-
-    @pl.loop(0, F_STEPS // 8)
-    def _(body):
-        value = degree_total[...]
-        for k in range(8):
-            n = body * 8 + k
-            held = [buf[rows_plan_s[0, n * GROUP + m]] for m in range(GROUP)]
-            marks = (held[0] + held[1]) + (held[2] + held[3])
-            here = lax.dot_general(ones, marks, OVER_COLS, preferred_element_type=f32)
-            value = value * rows_plan_s[2, n].astype(f32) + here[0:8]
-            degree_steps[n] = value
-        degree_total[...] = value
-        pl.when(body == 6)(lambda: gather(0, 6, 7, 10, 11))
-        pl.when(body == 16)(lambda: gather(0, 12, 13))
-
+    gather(0, 6, 7, 10, 11, 12, 13)
     gather_end(0)
 
     def tile_pass(plan_s, steps, product, hooks=()):
@@ -287,10 +272,10 @@
     tile_pass(
         rows_plan_s, F_STEPS, forward(0),
         hooks=(
-            (1, lambda: gather(1, 2, 3, 0, 1)),
-            (2, lambda: gather(1, 4, 5)),
+            (0, lambda: gather(1, 2, 3, 0, 1)),
+            (1, lambda: gather(1, 4, 5)),
             (4, lambda: gather(1, 8, 9)),
-            (6, lambda: gather(1, 6, 7, 10)),
+            (7, lambda: gather(1, 6, 7, 10)),
         ),
     )
     collect(rows_plan_s, ROW_TILES, partial.at[0])
@@ -341,15 +326,6 @@
         sum_near(h, 1)
 
     sum_start(0)
-
-    @pl.loop(0, ROW_TILES)
-    def _(n):
-        at = rows_plan_s[3, n]
-        degree[n] = degree_steps[jnp.maximum(at, 0)] * jnp.where(at >= 0, 1.0, 0.0)
-
-    for d in range(1, N_BLK):
-        to = (blk + d) & (N_BLK - 1)
-        links.send(S_DEGREE + d, degree.at[pl.ds(to * 4, 4)], degrees.at[d], blk_peer(d), degrees.at[0])
     gather(1, 11, 12, 13)
     gather_end(1)
     tile_pass(
@@ -362,19 +338,42 @@
     )
     collect(rows_plan_s, ROW_TILES, partial.at[1])
     sum_start(1)
-    sum_middle(1)
+
+    ones = jnp.ones((16, EDGE), bf16)
+    degree_total[...] = jnp.zeros_like(degree_total)
+
+    @pl.loop(0, F_STEPS // 8)
+    def _(body):
+        value = degree_total[...]
+        for k in range(8):
+            n = body * 8 + k
+            held = [buf[rows_plan_s[0, n * GROUP + m]] for m in range(GROUP)]
+            marks = (held[0] + held[1]) + (held[2] + held[3])
+            here = lax.dot_general(ones, marks, OVER_COLS, preferred_element_type=f32)
+            value = value * rows_plan_s[2, n].astype(f32) + here[0:8]
+            degree_steps[n] = value
+        degree_total[...] = value
+        pl.when(body == DEGREE_MIDDLE)(lambda: sum_middle(1))
+
+    @pl.loop(0, ROW_TILES)
+    def _(n):
+        at = rows_plan_s[3, n]
+        degree[n] = degree_steps[jnp.maximum(at, 0)] * jnp.where(at >= 0, 1.0, 0.0)
+
+    for d in range(1, N_BLK):
+        to = (blk + d) & (N_BLK - 1)
+        links.send(S_DEGREE + d, degree.at[pl.ds(to * 4, 4)], degrees.at[d], blk_peer(d), degrees.at[0])
     sum_combine(1, 1)
+    sum_across(1)
     for copy in node_loads:
         copy.wait()
+    self_term[...] = jnp.dot(feats[...], w_self[...], preferred_element_type=f32) + bias[...]
     for d in range(1, N_BLK):
         links.arrived(S_DEGREE + d, degrees.at[d])
     degree_sum = degree[pl.ds(blk * 4, 4)]
     for d in range(1, N_BLK):
         degree_sum += degrees[d]
     divisor = jnp.maximum(degree_sum, 1.0)
-    from_self = jnp.dot(feats[...], w_self[...], preferred_element_type=f32) + bias[...]
-    self_term[...] = from_self
-    sum_across(1)
 
     def grads_at(h, dy, j, half):
         return grads[h].at[pl.ds(blk_block(dy, j) * 4 + 2 * half, 2)]
@@ -407,9 +406,10 @@
         grads[h][block] = own_grads[h]
         links.send(sem(h, S_GRADS, 12), own_grads.at[h], grads[h].at[block], far_x, chunk_like)
 
-    def grads_along(h, j):
+    def grads_along(h, j, first=True, second=True):
         base = 6 * (1 - j)
-        for k, half, where in ((0, 0, y_up), (1, 1, y_down), (3, 1, y_up), (2, 0, y_down)):
+        ways = ((0, 0, y_up), (1, 1, y_down)) * first + ((3, 1, y_up), (2, 0, y_down)) * second
+        for k, half, where in ways:
             piece = grads_at(h, 0, j, half)
             links.send(sem(h, S_GRADS, base + k), piece, piece, where, piece_like)
 
@@ -463,6 +463,7 @@
         links.send(S_REP + d, rep_sum.at[(chip + d) & (N_CHIPS - 1)], rep_in.at[d], chip_peer(d), rep_in.at[0])
     rep_in[0] = rep_sum[chip]
     grads_other(0)
+    grads_along(1, 1, second=False)
     self_term[...] = lax.dot_general(d_pre[...], w_self[...], OVER_COLS, preferred_element_type=f32)
 
     for d in range(1, N_CHIPS):
@@ -473,10 +474,11 @@
     blk_out[0:32] = summed[0:32].astype(bf16)
     blk_out[32:48] = two_rows(summed[32:33] + summed[33:34])
     grads_onward(0, 0)
+    grads_along(1, 1, first=False)
+    grads_other(1)
     for d in range(1, N_BLK):
         links.send(S_BLK + d, blk_out, blk_in.at[d], blk_peer(d), blk_in.at[0])
     blk_in[0] = blk_out[...]
-    grads_along(1, 1)
 
     def own_weights(d=0):
         return weight_grads.at[core, pl.ds(((chip - d) & (N_CHIPS - 1)) * 32, 32)]
@@ -511,10 +513,9 @@
     tile_pass(
         cols_plan_s, B_STEPS, backward(0),
         hooks=(
-            (0, lambda: grads_other(1)),
-            (1, lambda: grads_onward(1, 1)),
-            (2, weights_end),
-            (4, lambda: grads_onward(1, 0)),
+            (0, lambda: grads_onward(1, 1)),
+            (3, lambda: grads_onward(1, 0)),
+            (5, weights_end),
         ),
     )
     collect(cols_plan_s, COL_TILES, back.at[0])

time: 114 us -> 110 us (0.965); the launches traced: 113 us -> 110 us
  Pallas kernels: 111 us -> 109 us
    pallas_call x1, Pallas kernels: 109 us -> 107 us  [local(): pl.pallas_call(layer_kernel, out_shape=(shaped((span, width), bf16), shap...]
where the time goes in v6:
time: 110 us
  Pallas kernels  109 us (99%)
  between operations  1.29 us (1%)
    pallas_call x1, Pallas kernels, local(): pl.pallas_call(layer_kernel, out_shape=(shaped((span, width), bf16), shap...  107 us

profile of v6, /device:TPU:2, one launch (start us, length us, event | category | flops | bytes accessed | tf_op | source)
XLA Modules:
  0.0 109.8 jit_solution(1349027304535090026)
XLA Ops:
  1.3 106.5 %shard_map.128 = (bf16[512,256]{1,0:T(8,128)(2,1)}, bf16[512,256]{1,0:T(8,128)(2,1)}, f32[2,256,256]{2,1,0:T(8,128)}, f32[8,256]{1,0:T(8,128)}) custom-call(bf16[512,256]{1,0:T(8,128)(2,1)} %features.1, bf16[4,128,256]{2,1,0:T(8,128)(2,1)} %bitcast.7, bf16[512,128,128]{2,1,0:T(8,128)(2,1)} %bitcast.6, s32[1,512]{1,0:T(1,128)} %bitcast.8, s32[1,512]{1,0:T(1,128)} %bitcast.9, ...), custom_call_target="tpu_custom_call" | custom-call | tf_op jit(solution)/shard_map/pallas_call | solution.py:650
  107.8 2.0 %shard_map.129 = (bf16[512,256]{1,0:T(8,128)(2,1)}, bf16[512,256]{1,0:T(8,128)(2,1)}, f32[256,256]{1,0:T(8,128)}, f32[256,256]{1,0:T(8,128)}, f32[1,256]{1,0:T(1,128)}) custom-call(bf16[512,256]{1,0:T(8,128)(2,1)} %get-tuple-element.14.act, bf16[512,256]{1,0:T(8,128)(2,1)} %get-tuple-element.15.grad_features, f32[2,256,256]{2,1,0:T(8,128)} %get-tuple-element.16.weight_grads, ...), custom_call_target="tpu_custom_call" | custom-call | tf_op jit(solution)/shard_map/pallas_call | solution.py:721
